TPU v7x, 512 devices: a whole 4x8x8 slice. The times are simulated.
512 devices in a mesh: pipe: 64 (over z, y_hi, core), tensor: 8 (over y_lo, x).
Axes of the slice: x: 4, y: 8 (y_hi: 4, y_lo: 2; y = y_hi * 2 + y_lo), z: 8, core: 2. Of those that a mesh axis runs over, the one named last changes fastest.
Arguments:
- fwd_queries: bfloat16 [64, 352, 8192], P('pipe', None, 'tensor'), may hold values from -100 to 100, as said below
- fwd_kv: bfloat16 [64, 2, 352, 1024], P('pipe', None, None, 'tensor'), may hold values from -6 to 6
- fwd_resid: bfloat16 [64, 352, 8192], P('pipe', None, 'tensor'), may hold values from -6 to 6
- fwd_bounds: int32 [64], P('pipe'), may hold values from 1 to 351
- gain: bfloat16 [8192], P('tensor'), may hold values from 0.099609375 to 1.8984375
- stash_queries: bfloat16 [64, 352, 8192], P('pipe', None, 'tensor'), may hold values from -100 to 100, as said below
- stash_kv: bfloat16 [64, 2, 352, 1024], P('pipe', None, None, 'tensor'), may hold values from -6 to 6
- stash_bounds: int32 [64], P('pipe'), may hold values from 1 to 351
- grad_out: bfloat16 [64, 352, 8192], P('pipe', None, 'tensor'), may hold values from -6 to 6
Outputs:
- normed: bfloat16 [64, 352, 8192], P('pipe', None, 'tensor')
- grad_queries: bfloat16 [64, 352, 8192], P('pipe', None, 'tensor')
- grad_kv: bfloat16 [64, 2, 352, 1024], P('pipe', None, None, 'tensor')
Inputs may be any that keep to these rules, and one draw needn't show every extreme that they name: `fwd_queries`: queries reach at most 100 in magnitude. `stash_queries`: queries reach at most 100 in magnitude.
All inputs are finite; a program needn't handle non-finite values.
Results may differ from a plain program's by a relative error of at most 0.005.
Values may be sent and summed in bfloat16 or wider, within the bound.
No kernel may reach another device: no remote copies, remote signals or barrier semaphores. Data moves between devices by JAX's collectives and lax.ppermute only.
A program may use at most 64 MiB of HBM per device.

v0:
```python
import jax
import jax.numpy as jnp
from jax import lax
from jax.sharding import PartitionSpec as P

HD = 128
D = 8192


def shifted(shard, axis, by):
    peers = lax.axis_size(axis)
    return lax.ppermute(shard, axis, [(i, (i + by) % peers) for i in range(peers)])


def partner(value, axis, apart):
    mask = 2**apart
    pairs = [(source, source ^ mask) for source in range(lax.axis_size(axis))]
    return lax.ppermute(value, axis, pairs)


def visible_mask(tok, bound):
    rows = jnp.arange(tok, dtype=jnp.int32)[:, None]
    cols = jnp.arange(tok, dtype=jnp.int32)[None, :]
    return (cols <= rows) & ((cols >= bound) | (rows < bound))


def split_heads(queries, pairs):
    tok = queries.shape[0]
    kv_heads = pairs.shape[2] // HD
    group = queries.shape[1] // HD // kv_heads
    q_heads = queries.reshape(tok, kv_heads, group, HD)
    k_heads = pairs[0].reshape(tok, kv_heads, HD)
    v_heads = pairs[1].reshape(tok, kv_heads, HD)
    return (q_heads, k_heads, v_heads)


def probs_of(q_heads, k_heads, bound):
    tok = q_heads.shape[0]
    scores = jnp.einsum("iagd,jad->agij", q_heads, k_heads, preferred_element_type=jnp.float32)
    scores = scores * HD ** (-0.5)
    scores = jnp.where(visible_mask(tok, bound)[None, None], scores, -jnp.inf)
    top = jnp.max(scores, axis=-1, keepdims=True)
    weights = jnp.exp(scores - top)
    return weights / jnp.sum(weights, axis=-1, keepdims=True)


def backward_local(queries, pairs, bound, grads):
    tok = queries.shape[0]
    q_heads, k_heads, v_heads = split_heads(queries, pairs)
    probs = probs_of(q_heads, k_heads, bound)
    rounded = probs.astype(jnp.bfloat16)
    g_heads = grads.reshape(q_heads.shape)
    grad_v = jnp.einsum("agij,iagd->jad", rounded, g_heads, preferred_element_type=jnp.float32)
    grad_p = jnp.einsum("iagd,jad->agij", g_heads, v_heads, preferred_element_type=jnp.float32)
    grad_s = probs * (grad_p - jnp.sum(probs * grad_p, axis=-1, keepdims=True))
    grad_s = (grad_s * HD ** (-0.5)).astype(jnp.bfloat16)
    grad_q = jnp.einsum("agij,jad->iagd", grad_s, k_heads, preferred_element_type=jnp.float32)
    grad_k = jnp.einsum("agij,iagd->jad", grad_s, q_heads, preferred_element_type=jnp.float32)
    grad_q = grad_q.reshape(tok, queries.shape[1]).astype(jnp.bfloat16)
    grad_pair = jnp.stack([grad_k.reshape(tok, -1), grad_v.reshape(tok, -1)]).astype(jnp.bfloat16)
    return (grad_q[None], grad_pair[None])


def per_device(
    fwd_queries,
    fwd_kv,
    fwd_resid,
    fwd_bounds,
    gain,
    stash_queries,
    stash_kv,
    stash_bounds,
    grad_out,
):
    q_in, kv_in, r_in, b_in = shifted((fwd_queries, fwd_kv, fwd_resid, fwd_bounds), "pipe", 1)
    grads_in = shifted(grad_out, "pipe", -1)
    q_heads, k_heads, v_heads = split_heads(q_in[0], kv_in[0])
    probs = probs_of(q_heads, k_heads, b_in[0])
    rounded = probs.astype(jnp.bfloat16)
    mixed = jnp.einsum("agij,jad->iagd", rounded, v_heads, preferred_element_type=jnp.float32)
    handoff = (r_in[0].astype(jnp.float32) + mixed.reshape(r_in.shape[1:])).astype(jnp.bfloat16)
    handoff = lax.optimization_barrier(handoff).astype(jnp.float32)
    squares = lax.psum(jnp.sum(handoff * handoff, axis=1), "tensor")
    scale = lax.rsqrt(squares / D + 1e-05)
    normed = (handoff * scale[:, None] * gain.astype(jnp.float32)[None, :]).astype(jnp.bfloat16)[
        None
    ]
    top_bit = lax.axis_size("pipe").bit_length() - 2
    kept = partner((stash_queries, stash_kv, stash_bounds), "pipe", top_bit)
    grad_queries, grad_kv = backward_local(kept[0][0], kept[1][0], kept[2][0], grads_in[0])
    return (normed, grad_queries, grad_kv)


def solution(mesh):
    placed = (
        P("pipe", None, "tensor"),
        P("pipe", None, None, "tensor"),
        P("pipe", None, "tensor"),
        P("pipe"),
        P("tensor"),
        P("pipe", None, "tensor"),
        P("pipe", None, None, "tensor"),
        P("pipe"),
        P("pipe", None, "tensor"),
    )
    return jax.shard_map(
        per_device,
        mesh=mesh,
        in_specs=placed,
        out_specs=(
            P("pipe", None, "tensor"),
            P("pipe", None, "tensor"),
            P("pipe", None, None, "tensor"),
        ),
        check_vma=False,
    )
```

profile of v0, /device:TPU:112, one launch (start us, length us, event | category | flops | bytes accessed | tf_op | source)
XLA Modules:
  0.0 121.2 jit_solution(3084718550348206264)
XLA Ops:
  0.6 10.0 %collective-permute-start.6 = (bf16[1,352,1024]{2,1,0:T(8,128)(2,1)}, bf16[1,352,1024]{2,1,0:T(8,128)(2,1)S(1)}, u32[]{:S(2)}, u32[]{:S(2)}) collective-permute-start(bf16[1,352,1024]{2,1,0:T(8,128)(2,1)} %param.14), channel_id=1, source_target_pairs={{0,256},{8,264},{16,272},{24,280},{32,288},{40,296},{48,304},{56,3... | collective-permute-start | bytes 2162696 | tf_op jit(solution)/shard_map/ppermute | solution.py:18
  10.7 3.2 %collective-permute-start.7 = (bf16[1,352,1024]{2,1,0:T(8,128)(2,1)}, bf16[1,352,1024]{2,1,0:T(8,128)(2,1)S(1)}, u32[]{:S(2)}, u32[]{:S(2)}) collective-permute-start(bf16[1,352,1024]{2,1,0:T(8,128)(2,1)} %param.17), channel_id=1, source_target_pairs={{0,504},{8,0},{16,8},{24,16},{32,24},{40,32},{48,40},{56,48},{64,5... | collective-permute-start | bytes 2162696 | tf_op jit(solution)/shard_map/ppermute | solution.py:12
  13.9 2.2 %collective-permute-start.4 = (s32[1]{0:T(128)}, s32[1]{0:T(128)}, u32[]{:S(2)}, u32[]{:S(2)}) collective-permute-start(s32[1]{0:T(128)} %param.16), channel_id=1, source_target_pairs={{0,256},{8,264},{16,272},{24,280},{32,288},{40,296},{48,304},{56,3... | collective-permute-start | bytes 20 | tf_op jit(solution)/shard_map/ppermute | solution.py:18
  16.1 7.5 %collective-permute-start.5 = (bf16[1,2,352,128]{3,2,1,0:T(8,128)(2,1)}, bf16[1,2,352,128]{3,2,1,0:T(8,128)(2,1)S(1)}, u32[]{:S(2)}, u32[]{:S(2)}) collective-permute-start(bf16[1,2,352,128]{3,2,1,0:T(8,128)(2,1)} %param.15), channel_id=1, source_target_pairs={{0,256},{8,264},{16,272},{24,280},{32,288},{40,296},{48,304},{56,3... | collective-permute-start | bytes 540680 | tf_op jit(solution)/shard_map/ppermute | solution.py:18
  23.6 1.9 %collective-permute-start.1 = (s32[1]{0:T(128)}, s32[1]{0:T(128)}, u32[]{:S(2)}, u32[]{:S(2)}) collective-permute-start(s32[1]{0:T(128)} %param.12), channel_id=1, source_target_pairs={{0,8},{8,16},{16,24},{24,32},{32,40},{40,48},{48,56},{56,64},{64,7... | collective-permute-start | bytes 20 | tf_op jit(solution)/shard_map/ppermute | solution.py:12
  26.2 30.9 %collective-permute-done.4 = s32[1]{0:T(128)} collective-permute-done((s32[1]{0:T(128)}, s32[1]{0:T(128)}, u32[]{:S(2)}, u32[]{:S(2)}) %collective-permute-start.4) | collective-permute-done | bytes 36 | tf_op jit(solution)/shard_map/ppermute | solution.py:18
  57.1 1.9 %collective-permute-start.2 = (bf16[1,2,352,128]{3,2,1,0:T(8,128)(2,1)}, bf16[1,2,352,128]{3,2,1,0:T(8,128)(2,1)S(1)}, u32[]{:S(2)}, u32[]{:S(2)}) collective-permute-start(bf16[1,2,352,128]{3,2,1,0:T(8,128)(2,1)} %param.10), channel_id=1, source_target_pairs={{0,8},{8,16},{16,24},{24,32},{32,40},{40,48},{48,56},{56,64},{64,7... | collective-permute-start | bytes 540680 | tf_op jit(solution)/shard_map/ppermute | solution.py:12
  59.6 1.9 %collective-permute-start.3 = (bf16[1,352,1024]{2,1,0:T(8,128)(2,1)}, bf16[1,352,1024]{2,1,0:T(8,128)(2,1)}, u32[]{:S(2)}, u32[]{:S(2)}) collective-permute-start(bf16[1,352,1024]{2,1,0:T(8,128)(2,1)} %param.9), channel_id=1, source_target_pairs={{0,8},{8,16},{16,24},{24,32},{32,40},{40,48},{48,56},{56,64},{64,7... | collective-permute-start | bytes 2162696 | tf_op jit(solution)/shard_map/ppermute | solution.py:12
  62.5 1.9 %collective-permute-start = (bf16[1,352,1024]{2,1,0:T(8,128)(2,1)}, bf16[1,352,1024]{2,1,0:T(8,128)(2,1)}, u32[]{:S(2)}, u32[]{:S(2)}) collective-permute-start(bf16[1,352,1024]{2,1,0:T(8,128)(2,1)} %param.11), channel_id=1, source_target_pairs={{0,8},{8,16},{16,24},{24,32},{32,40},{40,48},{48,56},{56,64},{64,7... | collective-permute-start | bytes 2162696 | tf_op jit(solution)/shard_map/ppermute | solution.py:12
  64.8 0.9 fusion.8
  65.7 1.0 fusion.6
  66.7 1.6 %fusion = (f32[8,352]{1,0:T(8,128)S(1)}, f32[352,352,8]{1,0,2:T(8,128)S(1)}) fusion(f32[8,352]{1,0:T(8,128)S(1)} %fusion.6, f32[8,352]{1,0:T(8,128)S(1)} %get-tuple-element.5, f32[352,352,8]{1,0,2:T(8,128)S(1)} %get-tuple-element.6, pred[352,352]{0,1:T(8,128)(4,1)S(1)} %fusion.45, bf16[352,8,128]{2,1,0:T(8,128)(2,1)S(1)} %bitcast.173, ...), kind=kOutput, calls=%fused_computation.4 | convolution fusion | flops 259699968 | bytes 9272320 | tf_op jit(solution)/shard_map/iagd,jad->agij/dot_general | solution.py:54
  68.3 1.5 %fusion.9 = bf16[8,352,352]{1,2,0:T(8,128)(2,1)S(1)} fusion(f32[352,352,8]{1,0,2:T(8,128)S(1)} %get-tuple-element.8, f32[8,352]{1,0:T(8,128)S(1)} %get-tuple-element.7, f32[8,352]{1,0:T(8,128)S(1)} %fusion.6, f32[8,352]{1,0:T(8,128)S(1)} %get-tuple-element.5, f32[352,352,8]{1,0,2:T(8,128)S(1)} %get-tuple-element.6, pred[352,352]{0,1:T(8,128)(4,1)S(1)} %fusion.45), kind=kLoop, calls=%fused_computation.16 | loop fusion | flops 7929856 | bytes 10070016 | tf_op jit(solution)/shard_map/reshape.33
  70.7 1.1 copy.20
  71.8 2.1 %convert_element_type.69 = bf16[1,352,1024]{2,1,0:T(8,128)(2,1)} reshape(bf16[352,1,8,128]{3,2,0,1:T(8,128)(2,1)} %copy.20) | data formatting | bytes 1441792 | tf_op jit(solution)/shard_map/convert_element_type | solution.py:59
  73.9 15.6 %collective-permute-done.3 = bf16[1,352,1024]{2,1,0:T(8,128)(2,1)} collective-permute-done((bf16[1,352,1024]{2,1,0:T(8,128)(2,1)}, bf16[1,352,1024]{2,1,0:T(8,128)(2,1)}, u32[]{:S(2)}, u32[]{:S(2)}) %collective-permute-start.3) | collective-permute-done | bytes 720928 | tf_op jit(solution)/shard_map/ppermute | solution.py:12
  89.6 1.3 %copy.25 = bf16[44,8,8,128]{3,2,1,0:T(8,128)(2,1)S(1)} copy(bf16[44,8,8,128]{3,1,2,0:T(8,128)(2,1)} %bitcast.56) | data formatting | bytes 1441792
  91.6 0.9 fusion.7
  92.5 0.9 fusion.4
  93.4 1.4 %fusion.17 = f32[352,1,8,128]{3,0,2,1:T(8,128)S(1)} fusion(f32[8,352]{1,0:T(8,128)S(1)} %fusion.4, f32[8,352]{1,0:T(8,128)S(1)} %get-tuple-element.3, f32[352,352,8]{1,0,2:T(8,128)S(1)} %get-tuple-element.4, pred[352,352]{0,1:T(8,128)(4,1)S(1)} %fusion.46, bf16[1,2,352,128]{3,2,1,0:T(8,128)(2,1)S(1)} %collective-permute-done.2), kind=kOutput, calls=%fused_computation.25 | convolution fusion | flops 258711552 | bytes 6017024 | tf_op jit(solution)/shard_map/agij,jad->iagd/dot_general | solution.py:80
  95.8 1.6 %fusion.32 = bf16[1,1,352,128]{3,2,1,0:T(8,128)(2,1)S(1)} fusion(f32[8,352]{1,0:T(8,128)S(1)} %fusion.6, f32[8,352]{1,0:T(8,128)S(1)} %get-tuple-element.5, f32[352,352,8]{1,0,2:T(8,128)S(1)} %bitcast.166, pred[352,352]{0,1:T(8,128)(4,1)S(1)} %fusion.45, bf16[352,8,128]{2,1,0:T(8,128)(2,1)S(1)} %bitcast.174), kind=kOutput, calls=%fused_computation.37 | convolution fusion | flops 258756608 | bytes 4922368 | tf_op jit(solution)/shard_map/agij,iagd->jad/dot_general | solution.py:53
  97.4 1.5 %fusion.23 = bf16[352,1024]{1,0:T(8,128)(2,1)S(1)} fusion(f32[44,8,8,128]{3,2,1,0:T(8,128)S(1)} %bitcast.167, bf16[1,352,1024]{2,1,0:T(8,128)(2,1)} %collective-permute-done), kind=kLoop, calls=%fused_computation.30 | loop fusion | flops 1081344 | bytes 2883584 | tf_op jit(solution)/shard_map/convert_element_type | solution.py:81
  99.1 20.3 %psum.7 = f32[352]{0:T(512)S(1)} all-reduce(f32[352]{0:T(512)S(1)} %fusion.20), channel_id=1, replica_groups=mesh['pipe'=64,'tensor'=8] {'tensor'}, use_global_device_ids=true, to_apply=%region_3.4 | all-reduce | flops 352 | bytes 2816 | tf_op jit(solution)/shard_map/psum | solution.py:83
  120.1 1.1 fusion.36
  (30 shorter events, 5.9 us)
Async XLA Ops:
  0.6 61.9 %collective-permute-start.6 = (bf16[1,352,1024]{2,1,0:T(8,128)(2,1)}, bf16[1,352,1024]{2,1,0:T(8,128)(2,1)S(1)}, u32[]{:S(2)}, u32[]{:S(2)}) collective-permute-start(bf16[1,352,1024]{2,1,0:T(8,128)(2,1)} %param.14), channel_id=1, source_target_pairs={{0,256},{8,264},{16,272},{24,280},{32,288},{40,296},{48,304},{56,3... | collective-permute-start | bytes 2162696 | tf_op jit(solution)/shard_map/ppermute | solution.py:18
  10.7 54.0 %collective-permute-start.7 = (bf16[1,352,1024]{2,1,0:T(8,128)(2,1)}, bf16[1,352,1024]{2,1,0:T(8,128)(2,1)S(1)}, u32[]{:S(2)}, u32[]{:S(2)}) collective-permute-start(bf16[1,352,1024]{2,1,0:T(8,128)(2,1)} %param.17), channel_id=1, source_target_pairs={{0,504},{8,0},{16,8},{24,16},{32,24},{40,32},{48,40},{56,48},{64,5... | collective-permute-start | bytes 2162696 | tf_op jit(solution)/shard_map/ppermute | solution.py:12
  13.9 43.3 %collective-permute-start.4 = (s32[1]{0:T(128)}, s32[1]{0:T(128)}, u32[]{:S(2)}, u32[]{:S(2)}) collective-permute-start(s32[1]{0:T(128)} %param.16), channel_id=1, source_target_pairs={{0,256},{8,264},{16,272},{24,280},{32,288},{40,296},{48,304},{56,3... | collective-permute-start | bytes 20 | tf_op jit(solution)/shard_map/ppermute | solution.py:18
  16.1 48.7 %collective-permute-start.5 = (bf16[1,2,352,128]{3,2,1,0:T(8,128)(2,1)}, bf16[1,2,352,128]{3,2,1,0:T(8,128)(2,1)S(1)}, u32[]{:S(2)}, u32[]{:S(2)}) collective-permute-start(bf16[1,2,352,128]{3,2,1,0:T(8,128)(2,1)} %param.15), channel_id=1, source_target_pairs={{0,256},{8,264},{16,272},{24,280},{32,288},{40,296},{48,304},{56,3... | collective-permute-start | bytes 540680 | tf_op jit(solution)/shard_map/ppermute | solution.py:18
  23.6 36.0 %collective-permute-start.1 = (s32[1]{0:T(128)}, s32[1]{0:T(128)}, u32[]{:S(2)}, u32[]{:S(2)}) collective-permute-start(s32[1]{0:T(128)} %param.12), channel_id=1, source_target_pairs={{0,8},{8,16},{16,24},{24,32},{32,40},{40,48},{48,56},{56,64},{64,7... | collective-permute-start | bytes 20 | tf_op jit(solution)/shard_map/ppermute | solution.py:12
  57.1 34.4 %collective-permute-start.2 = (bf16[1,2,352,128]{3,2,1,0:T(8,128)(2,1)}, bf16[1,2,352,128]{3,2,1,0:T(8,128)(2,1)S(1)}, u32[]{:S(2)}, u32[]{:S(2)}) collective-permute-start(bf16[1,2,352,128]{3,2,1,0:T(8,128)(2,1)} %param.10), channel_id=1, source_target_pairs={{0,8},{8,16},{16,24},{24,32},{32,40},{40,48},{48,56},{56,64},{64,7... | collective-permute-start | bytes 540680 | tf_op jit(solution)/shard_map/ppermute | solution.py:12
  59.6 29.9 %collective-permute-start.3 = (bf16[1,352,1024]{2,1,0:T(8,128)(2,1)}, bf16[1,352,1024]{2,1,0:T(8,128)(2,1)}, u32[]{:S(2)}, u32[]{:S(2)}) collective-permute-start(bf16[1,352,1024]{2,1,0:T(8,128)(2,1)} %param.9), channel_id=1, source_target_pairs={{0,8},{8,16},{16,24},{24,32},{32,40},{40,48},{48,56},{56,64},{64,7... | collective-permute-start | bytes 2162696 | tf_op jit(solution)/shard_map/ppermute | solution.py:12
  62.5 34.8 %collective-permute-start = (bf16[1,352,1024]{2,1,0:T(8,128)(2,1)}, bf16[1,352,1024]{2,1,0:T(8,128)(2,1)}, u32[]{:S(2)}, u32[]{:S(2)}) collective-permute-start(bf16[1,352,1024]{2,1,0:T(8,128)(2,1)} %param.11), channel_id=1, source_target_pairs={{0,8},{8,16},{16,24},{24,32},{32,40},{40,48},{48,56},{56,64},{64,7... | collective-permute-start | bytes 2162696 | tf_op jit(solution)/shard_map/ppermute | solution.py:12
  64.8 1.9 %copy-start.1 = (bf16[44,8,8,128]{3,2,1,0:T(8,128)(2,1)}, bf16[44,8,8,128]{3,2,1,0:T(8,128)(2,1)S(1)}, u32[]{:S(2)}) copy-start(bf16[44,8,8,128]{3,2,1,0:T(8,128)(2,1)S(1)} %copy.28) | copy-start | bytes 2162692
  65.7 2.6 %copy-start = (f32[352,352,8]{1,0,2:T(8,128)}, f32[352,352,8]{1,0,2:T(8,128)S(1)}, u32[]{:S(2)}) copy-start(f32[352,352,8]{1,0,2:T(8,128)S(1)} %get-tuple-element.6) | copy-start | bytes 11894788
  92.5 3.2 %slice-start = ((s8[4325376]{0:T(1024)(128)(4,1)}), s8[131072]{0:T(1024)(128)(4,1)S(1)}, s32[]{:S(2)}) async-start(s8[4325376]{0:T(1024)(128)(4,1)} %bitcast.165), calls=%async_computation | async-start | bytes 262144
  93.4 2.3 %slice-start.1 = ((s8[4325376]{0:T(1024)(128)(4,1)}), s8[4194304]{0:T(1024)(128)(4,1)S(1)}, s32[]{:S(2)}) async-start(s8[4325376]{0:T(1024)(128)(4,1)} %bitcast.165), calls=%async_computation.1 | async-start | bytes 8388608
  93.4 2.4 %copy-start.2 = (bf16[44,8,8,128]{3,2,1,0:T(8,128)(2,1)S(1)}, bf16[44,8,8,128]{3,2,1,0:T(8,128)(2,1)}, u32[]{:S(2)}) copy-start(bf16[44,8,8,128]{3,2,1,0:T(8,128)(2,1)} %copy-done.1) | copy-start | bytes 2162692
where the time goes:
time: 122 us; the launch traced here: 121 us
  waiting for transfers between devices  46.5 us (38%)
  starting transfers between devices  30.6 us (25%)
  blocking collectives  20.3 us (17%)
  other arithmetic  9.09 us (7%)
  matrix products  7.92 us (6%)
  local copies, waits for them, and re-layouts  5.76 us (5%)
    ppermute x3, waiting for transfers between devices, partner(): return lax.ppermute(value, axis, pairs)  30.9 us
    psum x1, blocking collectives, per_device(): squares = lax.psum(jnp.sum(handoff * handoff, axis=1), 'tensor')  20.3 us
    ppermute x3, starting transfers between devices, partner(): return lax.ppermute(value, axis, pairs)  19.8 us
    ppermute x5, waiting for transfers between devices, shifted(): lax.ppermute(shard, axis, [(i, (i + by) % peers) for i in range(peers)])  15.6 us
    ppermute x5, starting transfers between devices, shifted(): lax.ppermute(shard, axis, [(i, (i + by) % peers) for i in range(peers)])  10.9 us
    convert_element_type x2, local copies, waits for them, and re-layouts, backward_local(): grad_q = grad_q.reshape(tok, queries.shape[1]).astype(jnp.bfloat16)  3.26 us
  transfers between devices with their start and end apart: 8, of which 2 were waited for; matrix products, arithmetic and copies ran while one was open for 16% of the time, Pallas kernels for 0%

commit v1 on v0

v1 whole, which is shorter than its diff:
```python
import jax
import jax.numpy as jnp
from jax import lax
from jax.experimental import pallas as pl
from jax.experimental.pallas import tpu as pltpu
from jax.sharding import PartitionSpec as P

HD = 128
D = 8192
BLK = 128
LOG2E = 1.4426950408889634
NT = (((1,), (1,)), ((), ()))


def shifted(value, by):
    peers = lax.axis_size("pipe")
    return lax.ppermute(value, "pipe", [(i, (i + by) % peers) for i in range(peers)])


def partner(value):
    peers = lax.axis_size("pipe")
    return lax.ppermute(value, "pipe", [(i, i ^ (peers // 2)) for i in range(peers)])


def dot(a, b, dims=(((1,), (0,)), ((), ()))):
    return lax.dot_general(a, b, dims, preferred_element_type=jnp.float32)


def padded(block, rows):
    if block.shape[0] == rows:
        return block
    fill = jnp.zeros((rows - block.shape[0], block.shape[1]), block.dtype)
    return jnp.concatenate([block, fill], axis=0)


def bias_of(first, depth, bound):
    keys = lax.broadcasted_iota(jnp.int32, (depth, BLK), 0)
    rows = lax.broadcasted_iota(jnp.int32, (depth, BLK), 1) + first
    seen = (keys <= rows) & ((keys >= bound) | (rows < bound))
    return jnp.where(seen, 0.0, -jnp.inf).astype(jnp.float32)


def turned(block):
    return block.astype(jnp.float32).T.astype(jnp.bfloat16)


def probs_turned(keys, queries, bias):
    scores = dot(keys, queries, NT) + jnp.concatenate([bias, bias], axis=1)
    top = jnp.max(scores, axis=0, keepdims=True)
    weights = jnp.exp2((scores - top) * (LOG2E * HD**-0.5))
    return weights * (1.0 / jnp.sum(weights, axis=0, keepdims=True))


def stacked(ref, first, last):
    two = [padded(ref[first:last, h * HD : (h + 1) * HD], BLK) for h in range(2)]
    return jnp.concatenate(two, axis=0)


def spans(tok):
    return [(first, min(first + BLK, tok), first + BLK) for first in range(0, tok, BLK)]


def forward_kernel(b_ref, q_ref, kv_ref, r_ref, out_ref, sq_ref, k_pad, v_turned, bias_ref):
    tok = q_ref.shape[0]
    deep = k_pad.shape[0]

    @pl.when(pl.program_id(0) == 0)
    def _():
        k_pad[...] = padded(kv_ref[0], deep)
        v_turned[...] = turned(padded(kv_ref[1], deep))
        for n, (first, _, depth) in enumerate(spans(tok)):
            bias_ref[n, :depth] = bias_of(first, depth, b_ref[0])
        sq_ref[...] = jnp.zeros_like(sq_ref)

    for n, (first, last, depth) in enumerate(spans(tok)):
        probs = probs_turned(k_pad[:depth], stacked(q_ref, first, last), bias_ref[n, :depth])
        mixed = dot(v_turned[:, :depth], probs.astype(jnp.bfloat16))
        for h in range(2):
            cols = slice(h * HD, (h + 1) * HD)
            own = mixed[:, cols].T[: last - first]
            handoff = (r_ref[first:last, cols].astype(jnp.float32) + own).astype(jnp.bfloat16)
            out_ref[first:last, cols] = handoff
            wide = handoff.astype(jnp.float32)
            sq_ref[first:last] += wide * wide


def forward_local(queries, pairs, resid, bound):
    tok, width = queries.shape
    deep = -(-tok // BLK) * BLK
    two = pl.BlockSpec((tok, 2 * HD), lambda i: (0, i))
    return pl.pallas_call(
        forward_kernel,
        grid=(width // (2 * HD),),
        in_specs=[
            pl.BlockSpec(memory_space=pltpu.SMEM),
            two,
            pl.BlockSpec((2, tok, HD), lambda i: (0, 0, 0)),
            two,
        ],
        out_specs=[two, pl.BlockSpec((tok, HD), lambda i: (0, 0))],
        out_shape=[
            jax.ShapeDtypeStruct((tok, width), jnp.bfloat16),
            jax.ShapeDtypeStruct((tok, HD), jnp.float32),
        ],
        scratch_shapes=[
            pltpu.VMEM((deep, HD), jnp.bfloat16),
            pltpu.VMEM((HD, deep), jnp.bfloat16),
            pltpu.VMEM((deep // BLK, deep, BLK), jnp.float32),
        ],
        compiler_params=pltpu.CompilerParams(vmem_limit_bytes=32 * 2**20),
        cost_estimate=pl.CostEstimate(flops=6 * 10**8, bytes_accessed=3 * 10**6, transcendentals=10**6),
        name="forward",
    )(bound, queries, pairs, resid)


def backward_kernel(q_ref, kvb_ref, g_ref, dq_ref, dkv_ref, k_pad, v_pad, k_turned, bias_ref, dk_ref, dv_ref):
    tok = q_ref.shape[0]
    deep = k_pad.shape[0]

    @pl.when(pl.program_id(0) == 0)
    def _():
        k_pad[...] = padded(kvb_ref[:tok], deep)
        v_pad[...] = padded(kvb_ref[tok : 2 * tok], deep)
        k_turned[...] = turned(k_pad[...])
        digits = kvb_ref[2 * tok :].astype(jnp.float32)
        bound = (digits[0:1] * 16.0 + digits[8:9]).astype(jnp.int32)
        for n, (first, _, depth) in enumerate(spans(tok)):
            bias_ref[n, :depth] = bias_of(first, depth, bound)
        dk_ref[...] = jnp.zeros_like(dk_ref)
        dv_ref[...] = jnp.zeros_like(dv_ref)

    for n, (first, last, depth) in enumerate(spans(tok)):
        queries = stacked(q_ref, first, last)
        grads = stacked(g_ref, first, last)
        probs = probs_turned(k_pad[:depth], queries, bias_ref[n, :depth])
        dv_ref[:depth] += dot(probs.astype(jnp.bfloat16), grads)
        grad_p = dot(v_pad[:depth], grads, NT)
        total = jnp.sum(probs * grad_p, axis=0, keepdims=True)
        grad_s = (probs * (grad_p - total) * HD**-0.5).astype(jnp.bfloat16)
        dk_ref[:depth] += dot(grad_s, queries)
        grad_q = dot(k_turned[:, :depth], grad_s)
        for h in range(2):
            cols = slice(h * HD, (h + 1) * HD)
            dq_ref[first:last, cols] = grad_q[:, cols].T[: last - first].astype(jnp.bfloat16)

    @pl.when(pl.program_id(0) == pl.num_programs(0) - 1)
    def _():
        dkv_ref[0] = dk_ref[:tok].astype(jnp.bfloat16)
        dkv_ref[1] = dv_ref[:tok].astype(jnp.bfloat16)


def backward_local(queries, pairs_bound, grads):
    tok, width = queries.shape
    deep = -(-tok // BLK) * BLK
    two = pl.BlockSpec((tok, 2 * HD), lambda i: (0, i))
    return pl.pallas_call(
        backward_kernel,
        grid=(width // (2 * HD),),
        in_specs=[two, pl.BlockSpec(pairs_bound.shape, lambda i: (0, 0)), two],
        out_specs=[two, pl.BlockSpec((2, tok, HD), lambda i: (0, 0, 0))],
        out_shape=[
            jax.ShapeDtypeStruct((tok, width), jnp.bfloat16),
            jax.ShapeDtypeStruct((2, tok, HD), jnp.bfloat16),
        ],
        scratch_shapes=[
            pltpu.VMEM((deep, HD), jnp.bfloat16),
            pltpu.VMEM((deep, HD), jnp.bfloat16),
            pltpu.VMEM((HD, deep), jnp.bfloat16),
            pltpu.VMEM((deep // BLK, deep, BLK), jnp.float32),
            pltpu.VMEM((deep, HD), jnp.float32),
            pltpu.VMEM((deep, HD), jnp.float32),
        ],
        compiler_params=pltpu.CompilerParams(vmem_limit_bytes=32 * 2**20),
        cost_estimate=pl.CostEstimate(flops=15 * 10**8, bytes_accessed=3 * 10**6, transcendentals=10**6),
        name="backward",
    )(queries, pairs_bound, grads)


def with_bound(pairs, bound):
    high = lax.broadcasted_iota(jnp.int32, (16, HD), 0) < 8
    digits = jnp.where(high, bound[0] // 16, bound[0] % 16).astype(jnp.bfloat16)
    return jnp.concatenate([pairs.reshape(-1, HD), digits], axis=0)


def per_device(fwd_queries, fwd_kv, fwd_resid, fwd_bounds, gain, stash_queries, stash_kv, stash_bounds, grad_out):
    kept_q = partner(stash_queries[0])
    kept_kvb = partner(with_bound(stash_kv[0], stash_bounds))
    grads_in = shifted(grad_out[0], -1)
    handoff, squares = forward_local(fwd_queries[0], fwd_kv[0], fwd_resid[0], fwd_bounds)
    handed = shifted(handoff, 1)
    squares = lax.psum(jnp.sum(squares, axis=1), "tensor")
    scale = shifted(lax.rsqrt(squares / D + 1e-05), 1)
    normed = (handed.astype(jnp.float32) * scale[:, None] * gain.astype(jnp.float32)[None, :]).astype(jnp.bfloat16)
    grad_queries, grad_kv = backward_local(kept_q, kept_kvb, grads_in)
    return (normed[None], grad_queries[None], grad_kv[None])


def solution(mesh):
    placed = (
        P("pipe", None, "tensor"),
        P("pipe", None, None, "tensor"),
        P("pipe", None, "tensor"),
        P("pipe"),
        P("tensor"),
        P("pipe", None, "tensor"),
        P("pipe", None, None, "tensor"),
        P("pipe"),
        P("pipe", None, "tensor"),
    )
    return jax.shard_map(
        per_device,
        mesh=mesh,
        in_specs=placed,
        out_specs=(
            P("pipe", None, "tensor"),
            P("pipe", None, "tensor"),
            P("pipe", None, None, "tensor"),
        ),
        check_vma=False,
    )
```

time: 122 us -> 71.5 us (0.59)
  the two profiles are of different devices: /device:TPU:112 before, /device:TPU:120 now
where the time goes in v1:
time: 71.5 us; the launch traced here: 71.1 us
  starting transfers between devices  25.1 us (35%)
  blocking collectives  20 us (28%)
  Pallas kernels  11.1 us (16%)
  waiting for transfers between devices  8.19 us (11%)
  local copies, waits for them, and re-layouts  3.22 us (5%)
  between operations  2.05 us (3%)
  other arithmetic  1.42 us (2%)
    psum x1, blocking collectives, per_device(): squares = lax.psum(jnp.sum(squares, axis=1), 'tensor')  20 us
    ppermute x3, starting transfers between devices, shifted(): lax.ppermute(value, 'pipe', [(i, (i + by) % peers) for i in range(peers)])  12.9 us
    ppermute x2, starting transfers between devices, partner(): lax.ppermute(value, 'pipe', [(i, i ^ peers // 2) for i in range(peers)])  12.2 us
    ppermute x2, waiting for transfers between devices, partner(): lax.ppermute(value, 'pipe', [(i, i ^ peers // 2) for i in range(peers)])  8.18 us
    pallas_call x1, Pallas kernels, backward_local(): pl.pallas_call(backward_kernel, grid=(width // (2 * HD),), in_specs=[two,...  7.83 us
    pallas_call x1, Pallas kernels, forward_local(): pl.pallas_call(forward_kernel, grid=(width // (2 * HD),), in_specs=[pl.Bl...  3.3 us
    unnamed x10, local copies, waits for them, and re-layouts  3.14 us
  transfers between devices with their start and end apart: 5, of which 1 were waited for; matrix products, arithmetic and copies ran while one was open for 1% of the time, Pallas kernels for 16%

profile of v1, /device:TPU:120, one launch (start us, length us, event | category | flops | bytes accessed | tf_op | source)
XLA Modules:
  0.0 71.1 jit_solution(1034510602897328850)
XLA Ops:
  0.6 10.0 %collective-permute-start.2 = (bf16[352,1024]{1,0:T(8,128)(2,1)}, bf16[352,1024]{1,0:T(8,128)(2,1)S(1)}, u32[]{:S(2)}, u32[]{:S(2)}) collective-permute-start(bf16[352,1024]{1,0:T(8,128)(2,1)} %bitcast.19), channel_id=1, source_target_pairs={{0,256},{8,264},{16,272},{24,280},{32,288},{40,296},{48,304},{56,3... | collective-permute-start | bytes 2162696 | tf_op jit(solution)/shard_map/ppermute | solution.py:22
  10.7 3.2 %collective-permute-start.4 = (bf16[352,1024]{1,0:T(8,128)(2,1)}, bf16[352,1024]{1,0:T(8,128)(2,1)S(1)}, u32[]{:S(2)}, u32[]{:S(2)}) collective-permute-start(bf16[352,1024]{1,0:T(8,128)(2,1)} %bitcast.20), channel_id=1, source_target_pairs={{0,504},{8,0},{16,8},{24,16},{32,24},{40,32},{48,40},{56,48},{64,5... | collective-permute-start | bytes 2162696 | tf_op jit(solution)/shard_map/ppermute | solution.py:17
  14.5 0.0 copy-start
  14.5 1.1 %copy-done = bf16[1,352,1024]{2,1,0:T(8,128)(2,1)S(1)} copy-done((bf16[1,352,1024]{2,1,0:T(8,128)(2,1)S(1)}, bf16[1,352,1024]{2,1,0:T(8,128)(2,1)}, u32[]{:S(2)}) %copy-start) | copy-done | bytes 720920
  15.6 0.0 copy-start.1
  15.6 1.1 %copy-done.1 = bf16[1,352,1024]{2,1,0:T(8,128)(2,1)S(1)} copy-done((bf16[1,352,1024]{2,1,0:T(8,128)(2,1)S(1)}, bf16[1,352,1024]{2,1,0:T(8,128)(2,1)}, u32[]{:S(2)}) %copy-start.1) | copy-done | bytes 720920
  16.7 0.9 %copy-done.2 = bf16[1,2,352,128]{3,2,1,0:T(8,128)(2,1)S(1)} copy-done((bf16[1,2,352,128]{3,2,1,0:T(8,128)(2,1)S(1)}, bf16[1,2,352,128]{3,2,1,0:T(8,128)(2,1)}, u32[]{:S(2)}) %copy-start.2) | copy-done | bytes 180248
  17.7 3.3 %forward.1 = (bf16[352,1024]{1,0:T(8,128)(2,1)S(1)}, f32[352,128]{1,0:T(8,128)S(1)}) custom-call(s32[1]{0:T(128)S(6)} %copy.12.b_ref, bf16[352,1024]{1,0:T(8,128)(2,1)S(1)} %bitcast.15, bf16[2,352,128]{2,1,0:T(8,128)(2,1)S(1)} %bitcast.17, bf16[352,1024]{1,0:T(8,128)(2,1)S(1)} %bitcast.16), custom_call_target="tpu_custom_call" | custom-call | flops 600000000 | bytes 3000000 | tf_op jit(solution)/shard_map/forward/pallas_call | solution.py:91
  21.0 1.9 %collective-permute-start = (bf16[352,1024]{1,0:T(8,128)(2,1)S(1)}, bf16[352,1024]{1,0:T(8,128)(2,1)S(1)}, u32[]{:S(2)}, u32[]{:S(2)}) collective-permute-start(bf16[352,1024]{1,0:T(8,128)(2,1)S(1)} %get-tuple-element.7), channel_id=1, source_target_pairs={{0,8},{8,16},{16,24},{24,32},{32,40},{40,48},{48,56},{56,64},{64,7... | collective-permute-start | bytes 2162696 | tf_op jit(solution)/shard_map/ppermute | solution.py:17
  23.6 0.1 pad.1.clone
  23.7 0.0 copy-done.3
  23.7 0.2 pad_maximum_fusion
  23.8 2.2 %collective-permute-start.3 = (bf16[720,128]{1,0:T(8,128)(2,1)S(1)}, bf16[720,128]{1,0:T(8,128)(2,1)S(1)}, u32[]{:S(2)}, u32[]{:S(2)}) collective-permute-start(bf16[720,128]{1,0:T(8,128)(2,1)S(1)} %pad_maximum_fusion), channel_id=1, source_target_pairs={{0,256},{8,264},{16,272},{24,280},{32,288},{40,296},{48,304},{56,3... | collective-permute-start | bytes 552968 | tf_op jit(solution)/shard_map/ppermute | solution.py:22
  26.0 0.1 reduce_sum.9
  26.2 20.0 %psum.7 = f32[352]{0:T(512)S(1)} all-reduce(f32[352]{0:T(512)S(1)} %reduce_sum.9), channel_id=1, replica_groups=mesh['pipe'=64,'tensor'=8] {'tensor'}, use_global_device_ids=true, to_apply=%region_1.2 | all-reduce | flops 352 | bytes 2816 | tf_op jit(solution)/shard_map/psum | solution.py:191
  46.2 7.8 %collective-permute-start.1 = (f32[352]{0:T(512)S(1)}, f32[352]{0:T(512)S(1)}, u32[]{:S(2)}, u32[]{:S(2)}) collective-permute-start(f32[352]{0:T(512)S(1)} %add_rsqrt_fusion), channel_id=1, source_target_pairs={{0,8},{8,16},{16,24},{24,32},{32,40},{40,48},{48,56},{56,64},{64,7... | collective-permute-start | bytes 4232 | tf_op jit(solution)/shard_map/ppermute | solution.py:17
  54.0 0.0 copy-done.4
  54.0 8.2 %collective-permute-done.3.kvb_ref = bf16[720,128]{1,0:T(8,128)(2,1)S(1)} collective-permute-done((bf16[720,128]{1,0:T(8,128)(2,1)S(1)}, bf16[720,128]{1,0:T(8,128)(2,1)S(1)}, u32[]{:S(2)}, u32[]{:S(2)}) %collective-permute-start.3) | collective-permute-done | bytes 184352 | tf_op jit(solution)/shard_map/ppermute | solution.py:22
  62.2 0.0 collective-permute-done.2.q_ref
  62.2 0.0 collective-permute-done.4.g_ref
  62.2 7.8 %backward.1 = (bf16[352,1024]{1,0:T(8,128)(2,1)}, bf16[2,352,128]{2,1,0:T(8,128)(2,1)}) custom-call(bf16[352,1024]{1,0:T(8,128)(2,1)S(1)} %collective-permute-done.2.q_ref, bf16[720,128]{1,0:T(8,128)(2,1)S(1)} %collective-permute-done.3.kvb_ref, bf16[352,1024]{1,0:T(8,128)(2,1)S(1)} %collective-permute-done.4.g_ref), custom_call_target="tpu_custom_call" | custom-call | flops 1500000000 | bytes 3000000 | tf_op jit(solution)/shard_map/backward/pallas_call | solution.py:156
  70.0 0.0 collective-permute-done.1
  70.0 0.0 collective-permute-done
  70.0 1.1 %fusion = bf16[1,352,1024]{2,1,0:T(8,128)(2,1)} fusion(bf16[352,1024]{1,0:T(8,128)(2,1)S(1)} %collective-permute-done, f32[1024]{0:T(1024)S(1)} %convert_element_type.14, f32[352]{0:T(512)S(1)} %collective-permute-done.1), kind=kLoop, calls=%fused_computation.1 | loop fusion | flops 1441792 | bytes 1447296 | tf_op jit(solution)/shard_map/broadcast_in_dim | solution.py:195
  (6 shorter events, 0.0 us)
Async XLA Ops:
  0.6 61.6 %collective-permute-start.2 = (bf16[352,1024]{1,0:T(8,128)(2,1)}, bf16[352,1024]{1,0:T(8,128)(2,1)S(1)}, u32[]{:S(2)}, u32[]{:S(2)}) collective-permute-start(bf16[352,1024]{1,0:T(8,128)(2,1)} %bitcast.19), channel_id=1, source_target_pairs={{0,256},{8,264},{16,272},{24,280},{32,288},{40,296},{48,304},{56,3... | collective-permute-start | bytes 2162696 | tf_op jit(solution)/shard_map/ppermute | solution.py:22
  10.7 51.5 %collective-permute-start.4 = (bf16[352,1024]{1,0:T(8,128)(2,1)}, bf16[352,1024]{1,0:T(8,128)(2,1)S(1)}, u32[]{:S(2)}, u32[]{:S(2)}) collective-permute-start(bf16[352,1024]{1,0:T(8,128)(2,1)} %bitcast.20), channel_id=1, source_target_pairs={{0,504},{8,0},{16,8},{24,16},{32,24},{40,32},{48,40},{56,48},{64,5... | collective-permute-start | bytes 2162696 | tf_op jit(solution)/shard_map/ppermute | solution.py:17
  14.5 1.1 %copy-start = (bf16[1,352,1024]{2,1,0:T(8,128)(2,1)S(1)}, bf16[1,352,1024]{2,1,0:T(8,128)(2,1)}, u32[]{:S(2)}) copy-start(bf16[1,352,1024]{2,1,0:T(8,128)(2,1)} %param.9) | copy-start | bytes 2162692
  15.6 1.1 %copy-start.1 = (bf16[1,352,1024]{2,1,0:T(8,128)(2,1)S(1)}, bf16[1,352,1024]{2,1,0:T(8,128)(2,1)}, u32[]{:S(2)}) copy-start(bf16[1,352,1024]{2,1,0:T(8,128)(2,1)} %param.11) | copy-start | bytes 2162692
  16.7 0.9 %copy-start.2 = (bf16[1,2,352,128]{3,2,1,0:T(8,128)(2,1)S(1)}, bf16[1,2,352,128]{3,2,1,0:T(8,128)(2,1)}, u32[]{:S(2)}) copy-start(bf16[1,2,352,128]{3,2,1,0:T(8,128)(2,1)} %param.10) | copy-start | bytes 540676
  17.7 6.0 %copy-start.3 = (bf16[1,2,352,128]{3,2,1,0:T(8,128)(2,1)S(1)}, bf16[1,2,352,128]{3,2,1,0:T(8,128)(2,1)}, u32[]{:S(2)}) copy-start(bf16[1,2,352,128]{3,2,1,0:T(8,128)(2,1)} %param.15) | copy-start | bytes 540676
  17.7 36.3 %copy-start.4 = (bf16[1024]{0:T(1024)(128)(2,1)S(1)}, bf16[1024]{0:T(1024)(128)(2,1)}, u32[]{:S(2)}) copy-start(bf16[1024]{0:T(1024)(128)(2,1)} %param.13) | copy-start | bytes 6148
  21.0 49.1 %collective-permute-start = (bf16[352,1024]{1,0:T(8,128)(2,1)S(1)}, bf16[352,1024]{1,0:T(8,128)(2,1)S(1)}, u32[]{:S(2)}, u32[]{:S(2)}) collective-permute-start(bf16[352,1024]{1,0:T(8,128)(2,1)S(1)} %get-tuple-element.7), channel_id=1, source_target_pairs={{0,8},{8,16},{16,24},{24,32},{32,40},{40,48},{48,56},{56,64},{64,7... | collective-permute-start | bytes 2162696 | tf_op jit(solution)/shard_map/ppermute | solution.py:17
  23.8 38.4 %collective-permute-start.3 = (bf16[720,128]{1,0:T(8,128)(2,1)S(1)}, bf16[720,128]{1,0:T(8,128)(2,1)S(1)}, u32[]{:S(2)}, u32[]{:S(2)}) collective-permute-start(bf16[720,128]{1,0:T(8,128)(2,1)S(1)} %pad_maximum_fusion), channel_id=1, source_target_pairs={{0,256},{8,264},{16,272},{24,280},{32,288},{40,296},{48,304},{56,3... | collective-permute-start | bytes 552968 | tf_op jit(solution)/shard_map/ppermute | solution.py:22
  46.2 23.8 %collective-permute-start.1 = (f32[352]{0:T(512)S(1)}, f32[352]{0:T(512)S(1)}, u32[]{:S(2)}, u32[]{:S(2)}) collective-permute-start(f32[352]{0:T(512)S(1)} %add_rsqrt_fusion), channel_id=1, source_target_pairs={{0,8},{8,16},{16,24},{24,32},{32,40},{40,48},{48,56},{56,64},{64,7... | collective-permute-start | bytes 4232 | tf_op jit(solution)/shard_map/ppermute | solution.py:17

commit v2 on v1

v2 whole, which is shorter than its diff:
```python
import jax
import jax.numpy as jnp
from jax import lax
from jax.experimental import pallas as pl
from jax.experimental.pallas import tpu as pltpu
from jax.sharding import PartitionSpec as P

HD = 128
D = 8192
BLK = 128
GROUP = 8
LOG2E = 1.4426950408889634
NT = (((1,), (1,)), ((), ()))


def shifted(value, by):
    peers = lax.axis_size("pipe")
    return lax.ppermute(value, "pipe", [(i, (i + by) % peers) for i in range(peers)])


def partner(value):
    peers = lax.axis_size("pipe")
    return lax.ppermute(value, "pipe", [(i, i ^ (peers // 2)) for i in range(peers)])


def dot(a, b, dims=(((1,), (0,)), ((), ()))):
    return lax.dot_general(a, b, dims, preferred_element_type=jnp.float32)


def padded(block, rows):
    if block.shape[0] == rows:
        return block
    fill = jnp.zeros((rows - block.shape[0], block.shape[1]), block.dtype)
    return jnp.concatenate([block, fill], axis=0)


def bias_of(first, depth, bound):
    keys = lax.broadcasted_iota(jnp.int32, (depth, BLK), 0)
    rows = lax.broadcasted_iota(jnp.int32, (depth, BLK), 1) + first
    seen = (keys <= rows) & ((keys >= bound) | (rows < bound))
    return jnp.where(seen, 0.0, -jnp.inf).astype(jnp.float32)


def turned(block):
    return block.astype(jnp.float32).T.astype(jnp.bfloat16)


def weights_turned(keys, queries, bias):
    scores = dot(keys, queries, NT) + jnp.concatenate([bias] * GROUP, axis=1)
    top = jnp.max(scores, axis=0, keepdims=True)
    weights = jnp.exp2((scores - top) * (LOG2E * HD**-0.5))
    return weights, 1.0 / jnp.sum(weights, axis=0, keepdims=True)


def stacked(ref, start, first, last):
    heads = [padded(ref[first:last, (start + h) * HD : (start + h + 1) * HD], BLK) for h in range(GROUP)]
    return jnp.concatenate(heads, axis=0)


def bodies(tok, width):
    spans = [(first, min(first + BLK, tok), first + BLK) for first in range(0, tok, BLK)]
    return [span + (start,) for span in reversed(spans) for start in range(0, width // HD, GROUP)]


def forward_kernel(b_ref, q_far, kv_far, r_far, out_ref, sq_ref, q_ref, kv_ref, r_ref, sems):
    tok, width = q_ref.shape
    deep = -(-tok // BLK) * BLK
    near = [(kv_far, kv_ref), (q_far, q_ref), (r_far, r_ref)]
    copies = [pltpu.make_async_copy(src, dst, sems.at[n]) for n, (src, dst) in enumerate(near)]
    for copy in copies:
        copy.start()
    for copy in copies:
        copy.wait()
    keys = padded(kv_ref[0], deep)
    values = turned(padded(kv_ref[1], deep))
    biases = {}
    squares = {}
    for first, last, depth, start in bodies(tok, width):
        if first not in biases:
            biases[first] = bias_of(first, depth, b_ref[0])
        weights, inverse = weights_turned(keys[:depth], stacked(q_ref, start, first, last), biases[first])
        mixed = dot(values[:, :depth], (weights * inverse).astype(jnp.bfloat16))
        for h in range(GROUP):
            cols = slice((start + h) * HD, (start + h + 1) * HD)
            own = mixed[:, h * BLK : (h + 1) * BLK].T[: last - first]
            handoff = (r_ref[first:last, cols].astype(jnp.float32) + own).astype(jnp.bfloat16)
            out_ref[first:last, cols] = handoff
            wide = handoff.astype(jnp.float32)
            squares[first] = squares.get(first, 0.0) + wide * wide
    for first, square in squares.items():
        sq_ref[first : first + square.shape[0]] = square


def forward_local(queries, pairs, resid, bound):
    tok, width = queries.shape
    whole = pl.BlockSpec(memory_space=pltpu.VMEM)
    far = pl.BlockSpec(memory_space=pltpu.HBM)
    return pl.pallas_call(
        forward_kernel,
        in_specs=[pl.BlockSpec(memory_space=pltpu.SMEM), far, far, far],
        out_specs=[whole, whole],
        out_shape=[
            jax.ShapeDtypeStruct((tok, width), jnp.bfloat16),
            jax.ShapeDtypeStruct((tok, HD), jnp.float32),
        ],
        scratch_shapes=[
            pltpu.VMEM(queries.shape, jnp.bfloat16),
            pltpu.VMEM(pairs.shape, jnp.bfloat16),
            pltpu.VMEM(resid.shape, jnp.bfloat16),
            pltpu.SemaphoreType.DMA((3,)),
        ],
        compiler_params=pltpu.CompilerParams(vmem_limit_bytes=32 * 2**20),
        cost_estimate=pl.CostEstimate(flops=10**6, bytes_accessed=10**5, transcendentals=0),
        name="forward",
    )(bound, queries, pairs, resid)


def backward_kernel(q_ref, kvb_ref, g_ref, dq_ref, dkv_ref, dk_ref, dv_ref):
    tok, width = q_ref.shape
    deep = -(-tok // BLK) * BLK
    keys = padded(kvb_ref[:tok], deep)
    values = padded(kvb_ref[tok : 2 * tok], deep)
    keys_turned = turned(keys)
    digits = kvb_ref[2 * tok :].astype(jnp.float32)
    bound = (digits[0:1] * 16.0 + digits[8:9]).astype(jnp.int32)
    biases = {}
    for n, (first, last, depth, start) in enumerate(bodies(tok, width)):
        if first not in biases:
            biases[first] = bias_of(first, depth, bound)
        queries = stacked(q_ref, start, first, last)
        grads = stacked(g_ref, start, first, last)
        weights, inverse = weights_turned(keys[:depth], queries, biases[first])
        probs = weights * inverse
        own_v = dot(probs.astype(jnp.bfloat16), grads)
        grad_p = dot(values[:depth], grads, NT)
        total = jnp.sum(probs * grad_p, axis=0, keepdims=True)
        grad_s = (probs * (grad_p - total) * HD**-0.5).astype(jnp.bfloat16)
        own_k = dot(grad_s, queries)
        if n == 0:
            dv_ref[:depth] = own_v
            dk_ref[:depth] = own_k
        else:
            dv_ref[:depth] += own_v
            dk_ref[:depth] += own_k
        grad_q = dot(keys_turned[:, :depth], grad_s)
        for h in range(GROUP):
            cols = slice((start + h) * HD, (start + h + 1) * HD)
            dq_ref[first:last, cols] = grad_q[:, h * BLK : (h + 1) * BLK].T[: last - first].astype(jnp.bfloat16)
    dkv_ref[0] = dk_ref[:tok].astype(jnp.bfloat16)
    dkv_ref[1] = dv_ref[:tok].astype(jnp.bfloat16)


def backward_local(queries, pairs_bound, grads):
    tok, width = queries.shape
    deep = -(-tok // BLK) * BLK
    whole = pl.BlockSpec(memory_space=pltpu.VMEM)
    return pl.pallas_call(
        backward_kernel,
        in_specs=[whole, whole, whole],
        out_specs=[whole, whole],
        out_shape=[
            jax.ShapeDtypeStruct((tok, width), jnp.bfloat16),
            jax.ShapeDtypeStruct((2, tok, HD), jnp.bfloat16),
        ],
        scratch_shapes=[
            pltpu.VMEM((deep, HD), jnp.float32),
            pltpu.VMEM((deep, HD), jnp.float32),
        ],
        compiler_params=pltpu.CompilerParams(vmem_limit_bytes=32 * 2**20),
        cost_estimate=pl.CostEstimate(flops=10**11, bytes_accessed=3 * 10**6, transcendentals=10**6),
        name="backward",
    )(queries, pairs_bound, grads)


def with_bound(pairs, bound):
    high = lax.broadcasted_iota(jnp.int32, (16, HD), 0) < 8
    digits = jnp.where(high, bound[0] >> 4, bound[0] & 15).astype(jnp.bfloat16)
    return jnp.concatenate([pairs.reshape(-1, HD), digits], axis=0)


def summed(squares):
    peers = lax.axis_size("tensor")
    parts = jnp.broadcast_to(squares[None], (peers,) + squares.shape)
    return jnp.sum(lax.all_to_all(parts, "tensor", 0, 0), axis=0)


def per_device(fwd_queries, fwd_kv, fwd_resid, fwd_bounds, gain, stash_queries, stash_kv, stash_bounds, grad_out):
    kept_q = partner(stash_queries[0])
    handoff, squares = forward_local(fwd_queries[0], fwd_kv[0], fwd_resid[0], fwd_bounds)
    squares, grad_out = lax.optimization_barrier((squares, grad_out))
    grads_in = shifted(grad_out[0], -1)
    handed = shifted(handoff, 1)
    kept_kvb = partner(with_bound(stash_kv[0], stash_bounds))
    scale = shifted(lax.rsqrt(summed(jnp.sum(squares, axis=1)) / D + 1e-05), 1)
    grad_queries, grad_kv = backward_local(kept_q, kept_kvb, grads_in)
    handed, scale, grad_kv = lax.optimization_barrier((handed, scale, grad_kv))
    normed = (handed.astype(jnp.float32) * scale[:, None] * gain.astype(jnp.float32)[None, :]).astype(jnp.bfloat16)
    return (normed[None], grad_queries[None], grad_kv[None])


def solution(mesh):
    placed = (
        P("pipe", None, "tensor"),
        P("pipe", None, None, "tensor"),
        P("pipe", None, "tensor"),
        P("pipe"),
        P("tensor"),
        P("pipe", None, "tensor"),
        P("pipe", None, None, "tensor"),
        P("pipe"),
        P("pipe", None, "tensor"),
    )
    return jax.shard_map(
        per_device,
        mesh=mesh,
        in_specs=placed,
        out_specs=(
            P("pipe", None, "tensor"),
            P("pipe", None, "tensor"),
            P("pipe", None, None, "tensor"),
        ),
        check_vma=False,
    )
```

time: 71.5 us -> 67 us (0.937)
  the two profiles are of different devices: /device:TPU:120 before, /device:TPU:122 now
where the time goes in v2:
time: 67 us; the launch traced here: 66.6 us
  starting transfers between devices  35.3 us (53%)
  waiting for transfers between devices  17.1 us (26%)
  Pallas kernels  6.86 us (10%)
  local copies, waits for them, and re-layouts  3.83 us (6%)
  between operations  2.02 us (3%)
  other arithmetic  1.45 us (2%)
    ppermute x3, starting transfers between devices, shifted(): lax.ppermute(value, 'pipe', [(i, (i + by) % peers) for i in range(peers)])  17.4 us
    ppermute x2, waiting for transfers between devices, partner(): lax.ppermute(value, 'pipe', [(i, i ^ peers // 2) for i in range(peers)])  15.6 us
    ppermute x2, starting transfers between devices, partner(): lax.ppermute(value, 'pipe', [(i, i ^ peers // 2) for i in range(peers)])  12.2 us
    all_to_all x1, starting transfers between devices, summed(): return jnp.sum(lax.all_to_all(parts, 'tensor', 0, 0), axis=0)  5.73 us
    pallas_call x1, Pallas kernels, backward_local(): pl.pallas_call(backward_kernel, in_specs=[whole, whole, whole], out_specs...  4.02 us
    unnamed x10, local copies, waits for them, and re-layouts  3.14 us
    pallas_call x1, Pallas kernels, forward_local(): pl.pallas_call(forward_kernel, in_specs=[pl.BlockSpec(memory_space=pltpu....  2.84 us
    all_to_all x1, waiting for transfers between devices, summed(): return jnp.sum(lax.all_to_all(parts, 'tensor', 0, 0), axis=0)  1.53 us
  transfers between devices with their start and end apart: 6, of which 2 were waited for; matrix products, arithmetic and copies ran while one was open for 2% of the time, Pallas kernels for 10%

profile of v2, /device:TPU:122, one launch (start us, length us, event | category | flops | bytes accessed | tf_op | source)
XLA Modules:
  0.0 66.6 jit_solution(15588566665741158053)
XLA Ops:
  0.6 10.0 %collective-permute-start.2 = (bf16[352,1024]{1,0:T(8,128)(2,1)}, bf16[352,1024]{1,0:T(8,128)(2,1)S(1)}, u32[]{:S(2)}, u32[]{:S(2)}) collective-permute-start(bf16[352,1024]{1,0:T(8,128)(2,1)} %bitcast.16), channel_id=1, source_target_pairs={{0,256},{8,264},{16,272},{24,280},{32,288},{40,296},{48,304},{56,3... | collective-permute-start | bytes 2162696 | tf_op jit(solution)/shard_map/ppermute | solution.py:23
  11.3 1.1 %copy-done = bf16[1,352,1024]{2,1,0:T(8,128)(2,1)S(1)} copy-done((bf16[1,352,1024]{2,1,0:T(8,128)(2,1)S(1)}, bf16[1,352,1024]{2,1,0:T(8,128)(2,1)}, u32[]{:S(2)}) %copy-start) | copy-done | bytes 720920
  12.4 1.1 %copy-done.1 = bf16[1,352,1024]{2,1,0:T(8,128)(2,1)S(1)} copy-done((bf16[1,352,1024]{2,1,0:T(8,128)(2,1)S(1)}, bf16[1,352,1024]{2,1,0:T(8,128)(2,1)}, u32[]{:S(2)}) %copy-start.1) | copy-done | bytes 720920
  13.5 0.9 %copy-done.2 = bf16[1,2,352,128]{3,2,1,0:T(8,128)(2,1)S(1)} copy-done((bf16[1,2,352,128]{3,2,1,0:T(8,128)(2,1)S(1)}, bf16[1,2,352,128]{3,2,1,0:T(8,128)(2,1)}, u32[]{:S(2)}) %copy-start.2) | copy-done | bytes 180248
  14.4 2.8 %forward.1 = (bf16[352,1024]{1,0:T(8,128)(2,1)S(1)}, f32[352,128]{1,0:T(8,128)S(1)}) custom-call(s32[1]{0:T(128)S(6)} %copy.14.b_ref, bf16[352,1024]{1,0:T(8,128)(2,1)S(1)} %bitcast.12, bf16[2,352,128]{2,1,0:T(8,128)(2,1)S(1)} %bitcast.14, bf16[352,1024]{1,0:T(8,128)(2,1)S(1)} %bitcast.13), custom_call_target="tpu_custom_call" | custom-call | flops 1000000 | bytes 100000 | tf_op jit(solution)/shard_map/forward/pallas_call | solution.py:98
  17.3 3.2 %collective-permute-start.4 = (bf16[352,1024]{1,0:T(8,128)(2,1)}, bf16[352,1024]{1,0:T(8,128)(2,1)S(1)}, u32[]{:S(2)}, u32[]{:S(2)}) collective-permute-start(bf16[352,1024]{1,0:T(8,128)(2,1)} %bitcast.7), channel_id=1, source_target_pairs={{0,504},{8,0},{16,8},{24,16},{32,24},{40,32},{48,40},{56,48},{64,5... | collective-permute-start | bytes 2162696 | tf_op jit(solution)/shard_map/ppermute | solution.py:18
  20.5 1.9 %collective-permute-start = (bf16[352,1024]{1,0:T(8,128)(2,1)S(1)}, bf16[352,1024]{1,0:T(8,128)(2,1)S(1)}, u32[]{:S(2)}, u32[]{:S(2)}) collective-permute-start(bf16[352,1024]{1,0:T(8,128)(2,1)S(1)} %get-tuple-element.12), channel_id=1, source_target_pairs={{0,8},{8,16},{16,24},{24,32},{32,40},{40,48},{48,56},{56,64},{64,7... | collective-permute-start | bytes 2162696 | tf_op jit(solution)/shard_map/ppermute | solution.py:18
  22.4 0.1 reduce_sum.18
  22.6 0.6 broadcast_in_dim.25
  23.2 5.7 %all-to-all-start = ((f32[8,1,352]{2,1,0:T(1,128)}), f32[8,1,352]{2,1,0:T(1,128)S(1)}, u32[]{:S(2)}, u32[]{:S(2)}) async-start(f32[8,1,352]{2,1,0:T(1,128)} %broadcast_in_dim.25), calls=%async_computation | async-start | bytes 24576 | tf_op jit(solution)/shard_map/all_to_all | solution.py:184
  29.6 0.1 pad.1.clone
  29.7 0.0 copy-done.3
  29.7 0.2 pad_maximum_fusion
  29.8 2.2 %collective-permute-start.3 = (bf16[720,128]{1,0:T(8,128)(2,1)S(1)}, bf16[720,128]{1,0:T(8,128)(2,1)S(1)}, u32[]{:S(2)}, u32[]{:S(2)}) collective-permute-start(bf16[720,128]{1,0:T(8,128)(2,1)S(1)} %pad_maximum_fusion), channel_id=1, source_target_pairs={{0,256},{8,264},{16,272},{24,280},{32,288},{40,296},{48,304},{56,3... | collective-permute-start | bytes 552968 | tf_op jit(solution)/shard_map/ppermute | solution.py:23
  32.0 0.0 copy-done.4
  32.1 1.5 %all-to-all-done = f32[8,1,352]{2,1,0:T(1,128)S(1)} async-done(((f32[8,1,352]{2,1,0:T(1,128)}), f32[8,1,352]{2,1,0:T(1,128)S(1)}, u32[]{:S(2)}, u32[]{:S(2)}) %all-to-all-start) | async-done | bytes 11296 | tf_op jit(solution)/shard_map/all_to_all | solution.py:184
  33.6 12.3 %collective-permute-start.1 = (f32[352]{0:T(512)S(1)}, f32[352]{0:T(512)S(1)}, u32[]{:S(2)}, u32[]{:S(2)}) collective-permute-start(f32[352]{0:T(512)S(1)} %add_rsqrt_fusion), channel_id=1, source_target_pairs={{0,8},{8,16},{16,24},{24,32},{32,40},{40,48},{48,56},{56,64},{64,7... | collective-permute-start | bytes 4232 | tf_op jit(solution)/shard_map/ppermute | solution.py:18
  45.9 15.6 %collective-permute-done.3.kvb_ref = bf16[720,128]{1,0:T(8,128)(2,1)S(1)} collective-permute-done((bf16[720,128]{1,0:T(8,128)(2,1)S(1)}, bf16[720,128]{1,0:T(8,128)(2,1)S(1)}, u32[]{:S(2)}, u32[]{:S(2)}) %collective-permute-start.3) | collective-permute-done | bytes 184352 | tf_op jit(solution)/shard_map/ppermute | solution.py:23
  61.5 0.0 collective-permute-done.2.q_ref
  61.5 0.0 collective-permute-done.4.g_ref
  61.5 4.0 %backward.1 = (bf16[352,1024]{1,0:T(8,128)(2,1)}, bf16[2,352,128]{2,1,0:T(8,128)(2,1)}) custom-call(bf16[352,1024]{1,0:T(8,128)(2,1)S(1)} %collective-permute-done.2.q_ref, bf16[720,128]{1,0:T(8,128)(2,1)S(1)} %collective-permute-done.3.kvb_ref, bf16[352,1024]{1,0:T(8,128)(2,1)S(1)} %collective-permute-done.4.g_ref), custom_call_target="tpu_custom_call" | custom-call | flops 99999997952 | bytes 3000000 | tf_op jit(solution)/shard_map/backward/pallas_call | solution.py:157
  65.5 0.0 collective-permute-done.1
  65.5 0.0 collective-permute-done
  65.5 1.1 %fusion = bf16[1,352,1024]{2,1,0:T(8,128)(2,1)} fusion(bf16[352,1024]{1,0:T(8,128)(2,1)S(1)} %collective-permute-done, f32[1024]{0:T(1024)S(1)} %convert_element_type.15, f32[352]{0:T(512)S(1)} %collective-permute-done.1), kind=kLoop, calls=%fused_computation.1 | loop fusion | flops 1441792 | bytes 1447296 | tf_op jit(solution)/shard_map/broadcast_in_dim | solution.py:198
  (9 shorter events, 0.1 us)
Async XLA Ops:
  0.6 60.9 %collective-permute-start.2 = (bf16[352,1024]{1,0:T(8,128)(2,1)}, bf16[352,1024]{1,0:T(8,128)(2,1)S(1)}, u32[]{:S(2)}, u32[]{:S(2)}) collective-permute-start(bf16[352,1024]{1,0:T(8,128)(2,1)} %bitcast.16), channel_id=1, source_target_pairs={{0,256},{8,264},{16,272},{24,280},{32,288},{40,296},{48,304},{56,3... | collective-permute-start | bytes 2162696 | tf_op jit(solution)/shard_map/ppermute | solution.py:23
  11.3 1.1 %copy-start = (bf16[1,352,1024]{2,1,0:T(8,128)(2,1)S(1)}, bf16[1,352,1024]{2,1,0:T(8,128)(2,1)}, u32[]{:S(2)}) copy-start(bf16[1,352,1024]{2,1,0:T(8,128)(2,1)} %param.9) | copy-start | bytes 2162692
  12.4 1.1 %copy-start.1 = (bf16[1,352,1024]{2,1,0:T(8,128)(2,1)S(1)}, bf16[1,352,1024]{2,1,0:T(8,128)(2,1)}, u32[]{:S(2)}) copy-start(bf16[1,352,1024]{2,1,0:T(8,128)(2,1)} %param.11) | copy-start | bytes 2162692
  13.5 0.9 %copy-start.2 = (bf16[1,2,352,128]{3,2,1,0:T(8,128)(2,1)S(1)}, bf16[1,2,352,128]{3,2,1,0:T(8,128)(2,1)}, u32[]{:S(2)}) copy-start(bf16[1,2,352,128]{3,2,1,0:T(8,128)(2,1)} %param.10) | copy-start | bytes 540676
  14.4 15.2 %copy-start.3 = (bf16[1,2,352,128]{3,2,1,0:T(8,128)(2,1)S(1)}, bf16[1,2,352,128]{3,2,1,0:T(8,128)(2,1)}, u32[]{:S(2)}) copy-start(bf16[1,2,352,128]{3,2,1,0:T(8,128)(2,1)} %param.15) | copy-start | bytes 540676
  14.4 17.6 %copy-start.4 = (bf16[1024]{0:T(1024)(128)(2,1)S(1)}, bf16[1024]{0:T(1024)(128)(2,1)}, u32[]{:S(2)}) copy-start(bf16[1024]{0:T(1024)(128)(2,1)} %param.13) | copy-start | bytes 6148
  17.3 44.2 %collective-permute-start.4 = (bf16[352,1024]{1,0:T(8,128)(2,1)}, bf16[352,1024]{1,0:T(8,128)(2,1)S(1)}, u32[]{:S(2)}, u32[]{:S(2)}) collective-permute-start(bf16[352,1024]{1,0:T(8,128)(2,1)} %bitcast.7), channel_id=1, source_target_pairs={{0,504},{8,0},{16,8},{24,16},{32,24},{40,32},{48,40},{56,48},{64,5... | collective-permute-start | bytes 2162696 | tf_op jit(solution)/shard_map/ppermute | solution.py:18
  20.5 45.0 %collective-permute-start = (bf16[352,1024]{1,0:T(8,128)(2,1)S(1)}, bf16[352,1024]{1,0:T(8,128)(2,1)S(1)}, u32[]{:S(2)}, u32[]{:S(2)}) collective-permute-start(bf16[352,1024]{1,0:T(8,128)(2,1)S(1)} %get-tuple-element.12), channel_id=1, source_target_pairs={{0,8},{8,16},{16,24},{24,32},{32,40},{40,48},{48,56},{56,64},{64,7... | collective-permute-start | bytes 2162696 | tf_op jit(solution)/shard_map/ppermute | solution.py:18
  23.2 10.4 %all-to-all-start = ((f32[8,1,352]{2,1,0:T(1,128)}), f32[8,1,352]{2,1,0:T(1,128)S(1)}, u32[]{:S(2)}, u32[]{:S(2)}) async-start(f32[8,1,352]{2,1,0:T(1,128)} %broadcast_in_dim.25), calls=%async_computation | async-start | bytes 24576 | tf_op jit(solution)/shard_map/all_to_all | solution.py:184
  29.8 31.7 %collective-permute-start.3 = (bf16[720,128]{1,0:T(8,128)(2,1)S(1)}, bf16[720,128]{1,0:T(8,128)(2,1)S(1)}, u32[]{:S(2)}, u32[]{:S(2)}) collective-permute-start(bf16[720,128]{1,0:T(8,128)(2,1)S(1)} %pad_maximum_fusion), channel_id=1, source_target_pairs={{0,256},{8,264},{16,272},{24,280},{32,288},{40,296},{48,304},{56,3... | collective-permute-start | bytes 552968 | tf_op jit(solution)/shard_map/ppermute | solution.py:23
  33.6 31.9 %collective-permute-start.1 = (f32[352]{0:T(512)S(1)}, f32[352]{0:T(512)S(1)}, u32[]{:S(2)}, u32[]{:S(2)}) collective-permute-start(f32[352]{0:T(512)S(1)} %add_rsqrt_fusion), channel_id=1, source_target_pairs={{0,8},{8,16},{16,24},{24,32},{32,40},{40,48},{48,56},{56,64},{64,7... | collective-permute-start | bytes 4232 | tf_op jit(solution)/shard_map/ppermute | solution.py:18

commit v3 on v2

--- a/solution.py
+++ b/solution.py
@@ -115,56 +115,74 @@
     )(bound, queries, pairs, resid)
 
 
-def backward_kernel(q_ref, kvb_ref, g_ref, dq_ref, dkv_ref, dk_ref, dv_ref):
+def backward_kernel(
+    q_ref, kvb_ref, g_ref, dq_far, dkv_far, dq_ref, dkv_ref, dk_ref, dv_ref, sems
+):
     tok, width = q_ref.shape
-    deep = -(-tok // BLK) * BLK
+    deep = dk_ref.shape[0]
+    blocks = [block[:3] for block in bodies(tok, width) if block[3] == 0]
+    gone = []
+
+    def leave(source, target):
+        copy = pltpu.make_async_copy(source, target, sems.at[len(gone)])
+        copy.start()
+        gone.append(copy)
+
     keys = padded(kvb_ref[:tok], deep)
     values = padded(kvb_ref[tok : 2 * tok], deep)
     keys_turned = turned(keys)
     digits = kvb_ref[2 * tok :].astype(jnp.float32)
     bound = (digits[0:1] * 16.0 + digits[8:9]).astype(jnp.int32)
-    biases = {}
-    for n, (first, last, depth, start) in enumerate(bodies(tok, width)):
-        if first not in biases:
-            biases[first] = bias_of(first, depth, bound)
-        queries = stacked(q_ref, start, first, last)
-        grads = stacked(g_ref, start, first, last)
-        weights, inverse = weights_turned(keys[:depth], queries, biases[first])
-        probs = weights * inverse
-        own_v = dot(probs.astype(jnp.bfloat16), grads)
-        grad_p = dot(values[:depth], grads, NT)
-        total = jnp.sum(probs * grad_p, axis=0, keepdims=True)
-        grad_s = (probs * (grad_p - total) * HD**-0.5).astype(jnp.bfloat16)
-        own_k = dot(grad_s, queries)
-        if n == 0:
-            dv_ref[:depth] = own_v
-            dk_ref[:depth] = own_k
-        else:
-            dv_ref[:depth] += own_v
-            dk_ref[:depth] += own_k
-        grad_q = dot(keys_turned[:, :depth], grad_s)
-        for h in range(GROUP):
-            cols = slice((start + h) * HD, (start + h + 1) * HD)
-            dq_ref[first:last, cols] = grad_q[:, h * BLK : (h + 1) * BLK].T[: last - first].astype(jnp.bfloat16)
-    dkv_ref[0] = dk_ref[:tok].astype(jnp.bfloat16)
-    dkv_ref[1] = dv_ref[:tok].astype(jnp.bfloat16)
+    for n, (first, last, depth) in enumerate(blocks):
+        rows = pl.ds(first, last - first)
+        bias = bias_of(first, depth, bound)
+        for start in range(0, width // HD, GROUP):
+            queries = stacked(q_ref, start, first, last)
+            grads = stacked(g_ref, start, first, last)
+            weights, inverse = weights_turned(keys[:depth], queries, bias)
+            probs = weights * inverse
+            own_v = dot(probs.astype(jnp.bfloat16), grads)
+            grad_p = dot(values[:depth], grads, NT)
+            total = jnp.sum(probs * grad_p, axis=0, keepdims=True)
+            grad_s = (probs * (grad_p - total) * HD**-0.5).astype(jnp.bfloat16)
+            own_k = dot(grad_s, queries)
+            if n == 0 and start == 0:
+                dv_ref[:depth] = own_v
+                dk_ref[:depth] = own_k
+            else:
+                dv_ref[:depth] += own_v
+                dk_ref[:depth] += own_k
+            grad_q = dot(keys_turned[:, :depth], grad_s)
+            for h in range(GROUP):
+                cols = slice((start + h) * HD, (start + h + 1) * HD)
+                dq_ref[first:last, cols] = grad_q[:, h * BLK : (h + 1) * BLK].T[: last - first].astype(jnp.bfloat16)
+        dkv_ref[0, first:last] = dk_ref[first:last].astype(jnp.bfloat16)
+        dkv_ref[1, first:last] = dv_ref[first:last].astype(jnp.bfloat16)
+        leave(dq_ref.at[rows], dq_far.at[rows])
+        leave(dkv_ref.at[:, rows], dkv_far.at[:, rows])
+    for copy in gone:
+        copy.wait()
 
 
 def backward_local(queries, pairs_bound, grads):
     tok, width = queries.shape
     deep = -(-tok // BLK) * BLK
     whole = pl.BlockSpec(memory_space=pltpu.VMEM)
+    far = pl.BlockSpec(memory_space=pl.ANY)
     return pl.pallas_call(
         backward_kernel,
-        in_specs=[whole, whole, whole],
-        out_specs=[whole, whole],
+        in_specs=[whole] * 3,
+        out_specs=[far] * 2,
         out_shape=[
             jax.ShapeDtypeStruct((tok, width), jnp.bfloat16),
             jax.ShapeDtypeStruct((2, tok, HD), jnp.bfloat16),
         ],
         scratch_shapes=[
+            pltpu.VMEM((tok, width), jnp.bfloat16),
+            pltpu.VMEM((2, tok, HD), jnp.bfloat16),
             pltpu.VMEM((deep, HD), jnp.float32),
             pltpu.VMEM((deep, HD), jnp.float32),
+            pltpu.SemaphoreType.DMA((2 * (deep // BLK),)),
         ],
         compiler_params=pltpu.CompilerParams(vmem_limit_bytes=32 * 2**20),
         cost_estimate=pl.CostEstimate(flops=10**11, bytes_accessed=3 * 10**6, transcendentals=10**6),
@@ -176,6 +194,39 @@
     high = lax.broadcasted_iota(jnp.int32, (16, HD), 0) < 8
     digits = jnp.where(high, bound[0] >> 4, bound[0] & 15).astype(jnp.bfloat16)
     return jnp.concatenate([pairs.reshape(-1, HD), digits], axis=0)
+
+
+def finish_kernel(after_ref, handed_ref, scale_ref, gain_ref, far_ref, out_ref, sems):
+    del after_ref
+    tok = handed_ref.shape[0]
+    factor = gain_ref[...].astype(jnp.float32)
+    copies = []
+    for n, first in enumerate(range(0, tok, BLK)):
+        rows = slice(first, min(first + BLK, tok))
+        wide = handed_ref[rows].astype(jnp.float32) * scale_ref[rows] * factor
+        out_ref[rows] = wide.astype(jnp.bfloat16)
+        there = pl.ds(first, rows.stop - first)
+        copies.append(pltpu.make_async_copy(out_ref.at[there], far_ref.at[there], sems.at[n]))
+        copies[-1].start()
+    for copy in copies:
+        copy.wait()
+
+
+def finished(handed, scale, gain, after):
+    whole = pl.BlockSpec(memory_space=pltpu.VMEM)
+    return pl.pallas_call(
+        finish_kernel,
+        in_specs=[whole] * 4,
+        out_specs=pl.BlockSpec(memory_space=pl.ANY),
+        out_shape=jax.ShapeDtypeStruct(handed.shape, jnp.bfloat16),
+        scratch_shapes=[
+            pltpu.VMEM(handed.shape, jnp.bfloat16),
+            pltpu.SemaphoreType.DMA((-(-handed.shape[0] // BLK),)),
+        ],
+        compiler_params=pltpu.CompilerParams(vmem_limit_bytes=16 * 2**20),
+        cost_estimate=pl.CostEstimate(flops=10**9, bytes_accessed=0, transcendentals=0),
+        name="finish",
+    )(after, handed, scale, gain)
 
 
 def summed(squares):
@@ -192,9 +243,9 @@
     handed = shifted(handoff, 1)
     kept_kvb = partner(with_bound(stash_kv[0], stash_bounds))
     scale = shifted(lax.rsqrt(summed(jnp.sum(squares, axis=1)) / D + 1e-05), 1)
+    normed = finished(handed, scale[:, None], gain[None], kept_q)
+    normed, kept_kvb = lax.optimization_barrier((normed, kept_kvb))
     grad_queries, grad_kv = backward_local(kept_q, kept_kvb, grads_in)
-    handed, scale, grad_kv = lax.optimization_barrier((handed, scale, grad_kv))
-    normed = (handed.astype(jnp.float32) * scale[:, None] * gain.astype(jnp.float32)[None, :]).astype(jnp.bfloat16)
     return (normed[None], grad_queries[None], grad_kv[None])
 
 

time: 67 us -> 65.5 us (0.978)
  starting transfers between devices: 35.3 us -> 26.2 us
  waiting for transfers between devices: 17.1 us -> 24.8 us
  other arithmetic: 1.45 us -> 0.35 us
  Pallas kernels: 6.86 us -> 7.75 us
    ppermute x3, starting transfers between devices: 17.4 us -> 8.52 us  [shifted(): lax.ppermute(value, 'pipe', [(i, (i + by) % peers) for i in range(peers)])]
    ppermute x3, waiting for transfers between devices: 0.01 us -> 3.86 us  [shifted(): lax.ppermute(value, 'pipe', [(i, (i + by) % peers) for i in range(peers)])]
    all_to_all x1, waiting for transfers between devices: 1.53 us -> 3.96 us  [summed(): return jnp.sum(lax.all_to_all(parts, 'tensor', 0, 0), axis=0)]
    ppermute x2, waiting for transfers between devices: 15.6 us -> 17 us  [partner(): lax.ppermute(value, 'pipe', [(i, i ^ peers // 2) for i in range(peers)])]
    broadcast_in_dim x1 -> x0, other arithmetic: 1.09 us -> none  [per_device(): return (normed[None], grad_queries[None], grad_kv[None])]
    pallas_call x1 -> x2, Pallas kernels: 4.02 us -> 4.94 us  [the longest x1 3.93 us: backward_local(): pl.pallas_call(backward_kernel, in_specs=[whole] * 3, out_specs=[far] * 2...]
  transfers between devices with their start and end apart: 6 -> 6, of which waited for: 2 -> 4; matrix products, arithmetic and copies ran while one was open for 2% -> 2% of each run, Pallas kernels for 10% -> 6%
where the time goes in v3:
time: 65.5 us; the launch traced here: 65.1 us
  starting transfers between devices  26.2 us (40%)
  waiting for transfers between devices  24.8 us (38%)
  Pallas kernels  7.75 us (12%)
  local copies, waits for them, and re-layouts  3.94 us (6%)
  between operations  2.05 us (3%)
    ppermute x2, waiting for transfers between devices, partner(): lax.ppermute(value, 'pipe', [(i, i ^ peers // 2) for i in range(peers)])  17 us
    ppermute x2, starting transfers between devices, partner(): lax.ppermute(value, 'pipe', [(i, i ^ peers // 2) for i in range(peers)])  11.9 us
    ppermute x3, starting transfers between devices, shifted(): lax.ppermute(value, 'pipe', [(i, (i + by) % peers) for i in range(peers)])  8.52 us
    all_to_all x1, starting transfers between devices, summed(): return jnp.sum(lax.all_to_all(parts, 'tensor', 0, 0), axis=0)  5.73 us
    all_to_all x1, waiting for transfers between devices, summed(): return jnp.sum(lax.all_to_all(parts, 'tensor', 0, 0), axis=0)  3.96 us
    pallas_call x1, Pallas kernels, backward_local(): pl.pallas_call(backward_kernel, in_specs=[whole] * 3, out_specs=[far] * 2...  3.93 us
    ppermute x3, waiting for transfers between devices, shifted(): lax.ppermute(value, 'pipe', [(i, (i + by) % peers) for i in range(peers)])  3.86 us
    unnamed x10, local copies, waits for them, and re-layouts  3.14 us
  transfers between devices with their start and end apart: 6, of which 4 were waited for; matrix products, arithmetic and copies ran while one was open for 2% of the time, Pallas kernels for 6%

profile of v3, /device:TPU:122, one launch (start us, length us, event | category | flops | bytes accessed | tf_op | source)
XLA Modules:
  0.0 65.1 jit_solution(14669799714189585793)
XLA Ops:
  0.6 10.0 %collective-permute-start = (bf16[352,1024]{1,0:T(8,128)(2,1)}, bf16[352,1024]{1,0:T(8,128)(2,1)S(1)}, u32[]{:S(2)}, u32[]{:S(2)}) collective-permute-start(bf16[352,1024]{1,0:T(8,128)(2,1)} %bitcast.15), channel_id=1, source_target_pairs={{0,256},{8,264},{16,272},{24,280},{32,288},{40,296},{48,304},{56,3... | collective-permute-start | bytes 2162696 | tf_op jit(solution)/shard_map/ppermute | solution.py:23
  11.3 1.1 %copy-done = bf16[1,352,1024]{2,1,0:T(8,128)(2,1)S(1)} copy-done((bf16[1,352,1024]{2,1,0:T(8,128)(2,1)S(1)}, bf16[1,352,1024]{2,1,0:T(8,128)(2,1)}, u32[]{:S(2)}) %copy-start) | copy-done | bytes 720920
  12.4 1.1 %copy-done.1 = bf16[1,352,1024]{2,1,0:T(8,128)(2,1)S(1)} copy-done((bf16[1,352,1024]{2,1,0:T(8,128)(2,1)S(1)}, bf16[1,352,1024]{2,1,0:T(8,128)(2,1)}, u32[]{:S(2)}) %copy-start.1) | copy-done | bytes 720920
  13.5 0.9 %copy-done.2 = bf16[1,2,352,128]{3,2,1,0:T(8,128)(2,1)S(1)} copy-done((bf16[1,2,352,128]{3,2,1,0:T(8,128)(2,1)S(1)}, bf16[1,2,352,128]{3,2,1,0:T(8,128)(2,1)}, u32[]{:S(2)}) %copy-start.2) | copy-done | bytes 180248
  14.4 2.8 %forward.1 = (bf16[352,1024]{1,0:T(8,128)(2,1)S(1)}, f32[352,128]{1,0:T(8,128)S(1)}) custom-call(s32[1]{0:T(128)S(6)} %copy.17.b_ref, bf16[352,1024]{1,0:T(8,128)(2,1)S(1)} %bitcast.11, bf16[2,352,128]{2,1,0:T(8,128)(2,1)S(1)} %bitcast.13, bf16[352,1024]{1,0:T(8,128)(2,1)S(1)} %bitcast.12), custom_call_target="tpu_custom_call" | custom-call | flops 1000000 | bytes 100000 | tf_op jit(solution)/shard_map/forward/pallas_call | solution.py:98
  17.3 0.0 copy-start.3
  17.3 2.1 %collective-permute-start.1 = (bf16[352,1024]{1,0:T(8,128)(2,1)S(1)}, bf16[352,1024]{1,0:T(8,128)(2,1)S(1)}, u32[]{:S(2)}, u32[]{:S(2)}) collective-permute-start(bf16[352,1024]{1,0:T(8,128)(2,1)S(1)} %get-tuple-element.11), channel_id=1, source_target_pairs={{0,8},{8,16},{16,24},{24,32},{32,40},{40,48},{48,56},{56,64},{64,7... | collective-permute-start | bytes 2162696 | tf_op jit(solution)/shard_map/ppermute | solution.py:18
  19.3 4.5 %collective-permute-start.4 = (bf16[352,1024]{1,0:T(8,128)(2,1)}, bf16[352,1024]{1,0:T(8,128)(2,1)S(1)}, u32[]{:S(2)}, u32[]{:S(2)}) collective-permute-start(bf16[352,1024]{1,0:T(8,128)(2,1)} %bitcast.8), channel_id=1, source_target_pairs={{0,504},{8,0},{16,8},{24,16},{32,24},{40,32},{48,40},{56,48},{64,5... | collective-permute-start | bytes 2162696 | tf_op jit(solution)/shard_map/ppermute | solution.py:18
  23.9 0.1 reduce_sum.18
  24.0 0.6 broadcast_in_dim.29
  24.7 5.7 %all-to-all-start = ((f32[8,1,352]{2,1,0:T(1,128)}), f32[8,1,352]{2,1,0:T(1,128)S(1)}, u32[]{:S(2)}, u32[]{:S(2)}) async-start(f32[8,1,352]{2,1,0:T(1,128)} %broadcast_in_dim.29), calls=%async_computation | async-start | bytes 24576 | tf_op jit(solution)/shard_map/all_to_all | solution.py:235
  31.0 0.1 pad.1.clone
  31.1 0.2 pad_maximum_fusion
  31.3 1.9 %collective-permute-start.3 = (bf16[720,128]{1,0:T(8,128)(2,1)S(1)}, bf16[720,128]{1,0:T(8,128)(2,1)S(1)}, u32[]{:S(2)}, u32[]{:S(2)}) collective-permute-start(bf16[720,128]{1,0:T(8,128)(2,1)S(1)} %pad_maximum_fusion), channel_id=1, source_target_pairs={{0,256},{8,264},{16,272},{24,280},{32,288},{40,296},{48,304},{56,3... | collective-permute-start | bytes 552968 | tf_op jit(solution)/shard_map/ppermute | solution.py:23
  33.2 4.0 %all-to-all-done = f32[8,1,352]{2,1,0:T(1,128)S(1)} async-done(((f32[8,1,352]{2,1,0:T(1,128)}), f32[8,1,352]{2,1,0:T(1,128)S(1)}, u32[]{:S(2)}, u32[]{:S(2)}) %all-to-all-start) | async-done | bytes 11296 | tf_op jit(solution)/shard_map/all_to_all | solution.py:235
  37.2 1.9 %collective-permute-start.2 = (f32[352]{0:T(512)S(1)}, f32[352]{0:T(512)S(1)}, u32[]{:S(2)}, u32[]{:S(2)}) collective-permute-start(f32[352]{0:T(512)S(1)} %add_rsqrt_fusion), channel_id=1, source_target_pairs={{0,8},{8,16},{16,24},{24,32},{32,40},{40,48},{48,56},{56,64},{64,7... | collective-permute-start | bytes 4232 | tf_op jit(solution)/shard_map/ppermute | solution.py:18
  39.2 3.9 %collective-permute-done.2 = f32[352]{0:T(512)S(1)} collective-permute-done((f32[352]{0:T(512)S(1)}, f32[352]{0:T(512)S(1)}, u32[]{:S(2)}, u32[]{:S(2)}) %collective-permute-start.2) | collective-permute-done | bytes 1440 | tf_op jit(solution)/shard_map/ppermute | solution.py:18
  43.0 0.1 broadcast_in_dim.37.scale_ref
  43.1 14.9 %collective-permute-done.after_ref.q_ref = bf16[352,1024]{1,0:T(8,128)(2,1)S(1)} collective-permute-done((bf16[352,1024]{1,0:T(8,128)(2,1)}, bf16[352,1024]{1,0:T(8,128)(2,1)S(1)}, u32[]{:S(2)}, u32[]{:S(2)}) %collective-permute-start) | collective-permute-done | bytes 720928 | tf_op jit(solution)/shard_map/ppermute | solution.py:23
  58.0 0.0 collective-permute-done.1.handed_ref
  58.0 1.0 %finish.1 = bf16[352,1024]{1,0:T(8,128)(2,1)} custom-call(bf16[352,1024]{1,0:T(8,128)(2,1)S(1)} %collective-permute-done.after_ref.q_ref, bf16[352,1024]{1,0:T(8,128)(2,1)S(1)} %collective-permute-done.1.handed_ref, f32[352,1]{1,0:T(8,128)S(1)} %broadcast_in_dim.37.scale_ref, bf16[1,1024]{1,0:T(2,128)(2,1)S(1)} %broadcast_in_dim.31.gain_ref), custom_call_target="tpu_custom_call" | custom-call | flops 1000000000 | tf_op jit(solution)/shard_map/finish/pallas_call | solution.py:217
  59.0 2.1 %collective-permute-done.3.kvb_ref = bf16[720,128]{1,0:T(8,128)(2,1)S(1)} collective-permute-done((bf16[720,128]{1,0:T(8,128)(2,1)S(1)}, bf16[720,128]{1,0:T(8,128)(2,1)S(1)}, u32[]{:S(2)}, u32[]{:S(2)}) %collective-permute-start.3) | collective-permute-done | bytes 184352 | tf_op jit(solution)/shard_map/ppermute | solution.py:23
  61.2 0.0 collective-permute-done.4.g_ref
  61.2 3.9 %backward.1 = (bf16[352,1024]{1,0:T(8,128)(2,1)}, bf16[2,352,128]{2,1,0:T(8,128)(2,1)}) custom-call(bf16[352,1024]{1,0:T(8,128)(2,1)S(1)} %collective-permute-done.after_ref.q_ref, bf16[720,128]{1,0:T(8,128)(2,1)S(1)} %collective-permute-done.3.kvb_ref, bf16[352,1024]{1,0:T(8,128)(2,1)S(1)} %collective-permute-done.4.g_ref), custom_call_target="tpu_custom_call" | custom-call | flops 99999997952 | bytes 3000000 | tf_op jit(solution)/shard_map/backward/pallas_call | solution.py:172
  (10 shorter events, 0.1 us)
Async XLA Ops:
  0.6 57.4 %collective-permute-start = (bf16[352,1024]{1,0:T(8,128)(2,1)}, bf16[352,1024]{1,0:T(8,128)(2,1)S(1)}, u32[]{:S(2)}, u32[]{:S(2)}) collective-permute-start(bf16[352,1024]{1,0:T(8,128)(2,1)} %bitcast.15), channel_id=1, source_target_pairs={{0,256},{8,264},{16,272},{24,280},{32,288},{40,296},{48,304},{56,3... | collective-permute-start | bytes 2162696 | tf_op jit(solution)/shard_map/ppermute | solution.py:23
  11.3 1.1 %copy-start = (bf16[1,352,1024]{2,1,0:T(8,128)(2,1)S(1)}, bf16[1,352,1024]{2,1,0:T(8,128)(2,1)}, u32[]{:S(2)}) copy-start(bf16[1,352,1024]{2,1,0:T(8,128)(2,1)} %param.9) | copy-start | bytes 2162692
  12.4 1.1 %copy-start.1 = (bf16[1,352,1024]{2,1,0:T(8,128)(2,1)S(1)}, bf16[1,352,1024]{2,1,0:T(8,128)(2,1)}, u32[]{:S(2)}) copy-start(bf16[1,352,1024]{2,1,0:T(8,128)(2,1)} %param.11) | copy-start | bytes 2162692
  13.5 0.9 %copy-start.2 = (bf16[1,2,352,128]{3,2,1,0:T(8,128)(2,1)S(1)}, bf16[1,2,352,128]{3,2,1,0:T(8,128)(2,1)}, u32[]{:S(2)}) copy-start(bf16[1,2,352,128]{3,2,1,0:T(8,128)(2,1)} %param.10) | copy-start | bytes 540676
  17.3 13.9 %copy-start.3 = (bf16[1,2,352,128]{3,2,1,0:T(8,128)(2,1)S(1)}, bf16[1,2,352,128]{3,2,1,0:T(8,128)(2,1)}, u32[]{:S(2)}) copy-start(bf16[1,2,352,128]{3,2,1,0:T(8,128)(2,1)} %param.15) | copy-start | bytes 540676
  17.3 40.8 %collective-permute-start.1 = (bf16[352,1024]{1,0:T(8,128)(2,1)S(1)}, bf16[352,1024]{1,0:T(8,128)(2,1)S(1)}, u32[]{:S(2)}, u32[]{:S(2)}) collective-permute-start(bf16[352,1024]{1,0:T(8,128)(2,1)S(1)} %get-tuple-element.11), channel_id=1, source_target_pairs={{0,8},{8,16},{16,24},{24,32},{32,40},{40,48},{48,56},{56,64},{64,7... | collective-permute-start | bytes 2162696 | tf_op jit(solution)/shard_map/ppermute | solution.py:18
  19.3 41.8 %collective-permute-start.4 = (bf16[352,1024]{1,0:T(8,128)(2,1)}, bf16[352,1024]{1,0:T(8,128)(2,1)S(1)}, u32[]{:S(2)}, u32[]{:S(2)}) collective-permute-start(bf16[352,1024]{1,0:T(8,128)(2,1)} %bitcast.8), channel_id=1, source_target_pairs={{0,504},{8,0},{16,8},{24,16},{32,24},{40,32},{48,40},{56,48},{64,5... | collective-permute-start | bytes 2162696 | tf_op jit(solution)/shard_map/ppermute | solution.py:18
  24.7 12.5 %all-to-all-start = ((f32[8,1,352]{2,1,0:T(1,128)}), f32[8,1,352]{2,1,0:T(1,128)S(1)}, u32[]{:S(2)}, u32[]{:S(2)}) async-start(f32[8,1,352]{2,1,0:T(1,128)} %broadcast_in_dim.29), calls=%async_computation | async-start | bytes 24576 | tf_op jit(solution)/shard_map/all_to_all | solution.py:235
  31.3 29.9 %collective-permute-start.3 = (bf16[720,128]{1,0:T(8,128)(2,1)S(1)}, bf16[720,128]{1,0:T(8,128)(2,1)S(1)}, u32[]{:S(2)}, u32[]{:S(2)}) collective-permute-start(bf16[720,128]{1,0:T(8,128)(2,1)S(1)} %pad_maximum_fusion), channel_id=1, source_target_pairs={{0,256},{8,264},{16,272},{24,280},{32,288},{40,296},{48,304},{56,3... | collective-permute-start | bytes 552968 | tf_op jit(solution)/shard_map/ppermute | solution.py:23
  37.2 1.9 %copy-start.4 = (bf16[1024]{0:T(1024)(128)(2,1)S(1)}, bf16[1024]{0:T(1024)(128)(2,1)}, u32[]{:S(2)}) copy-start(bf16[1024]{0:T(1024)(128)(2,1)} %param.13) | copy-start | bytes 6148
  37.2 5.8 %collective-permute-start.2 = (f32[352]{0:T(512)S(1)}, f32[352]{0:T(512)S(1)}, u32[]{:S(2)}, u32[]{:S(2)}) collective-permute-start(f32[352]{0:T(512)S(1)} %add_rsqrt_fusion), channel_id=1, source_target_pairs={{0,8},{8,16},{16,24},{24,32},{32,40},{40,48},{48,56},{56,64},{64,7... | collective-permute-start | bytes 4232 | tf_op jit(solution)/shard_map/ppermute | solution.py:18

commit v4 on v3

--- a/solution.py
+++ b/solution.py
@@ -69,7 +69,7 @@
     copies = [pltpu.make_async_copy(src, dst, sems.at[n]) for n, (src, dst) in enumerate(near)]
     for copy in copies:
         copy.start()
-    for copy in copies:
+    for copy in copies[:-1]:
         copy.wait()
     keys = padded(kv_ref[0], deep)
     values = turned(padded(kv_ref[1], deep))
@@ -80,6 +80,8 @@
             biases[first] = bias_of(first, depth, b_ref[0])
         weights, inverse = weights_turned(keys[:depth], stacked(q_ref, start, first, last), biases[first])
         mixed = dot(values[:, :depth], (weights * inverse).astype(jnp.bfloat16))
+        if not squares:
+            copies[-1].wait()
         for h in range(GROUP):
             cols = slice((start + h) * HD, (start + h + 1) * HD)
             own = mixed[:, h * BLK : (h + 1) * BLK].T[: last - first]
@@ -109,7 +111,7 @@
             pltpu.VMEM(resid.shape, jnp.bfloat16),
             pltpu.SemaphoreType.DMA((3,)),
         ],
-        compiler_params=pltpu.CompilerParams(vmem_limit_bytes=32 * 2**20),
+        compiler_params=pltpu.CompilerParams(vmem_limit_bytes=56 * 2**20),
         cost_estimate=pl.CostEstimate(flops=10**6, bytes_accessed=10**5, transcendentals=0),
         name="forward",
     )(bound, queries, pairs, resid)

time: 65.5 us -> 65 us (level)
  local copies, waits for them, and re-layouts: 3.94 us -> 0.81 us
  Pallas kernels: 7.75 us -> 9.29 us
  other arithmetic: 0.35 us -> 1.27 us
    unnamed x10 -> x6, local copies, waits for them, and re-layouts: 3.14 us -> 0.01 us
    pallas_call x1, Pallas kernels: 2.82 us -> 4.36 us  [forward_local(): pl.pallas_call(forward_kernel, in_specs=[pl.BlockSpec(memory_space=pltpu....]
    ppermute x2, waiting for transfers between devices: 17 us -> 18.4 us  [partner(): lax.ppermute(value, 'pipe', [(i, i ^ peers // 2) for i in range(peers)])]
    all_to_all x1, waiting for transfers between devices: 3.96 us -> 2.77 us  [summed(): return jnp.sum(lax.all_to_all(parts, 'tensor', 0, 0), axis=0)]
    reduce_sum x1, other arithmetic: 0.14 us -> 1.07 us  [per_device(): scale = shifted(lax.rsqrt(summed(jnp.sum(squares, axis=1)) / D + 1e-05), 1)]
  transfers between devices with their start and end apart: 6 -> 6, of which waited for: 4 -> 4; matrix products, arithmetic and copies ran while one was open for 2% -> 3% of each run, Pallas kernels for 6% -> 8%
where the time goes in v4:
time: 65 us; the launch traced here: 64.6 us
  starting transfers between devices  26.2 us (40%)
  waiting for transfers between devices  25 us (38%)
  Pallas kernels  9.29 us (14%)
  between operations  2.06 us (3%)
  other arithmetic  1.27 us (2%)
  local copies, waits for them, and re-layouts  0.81 us (1%)
    ppermute x2, waiting for transfers between devices, partner(): lax.ppermute(value, 'pipe', [(i, i ^ peers // 2) for i in range(peers)])  18.4 us
    ppermute x2, starting transfers between devices, partner(): lax.ppermute(value, 'pipe', [(i, i ^ peers // 2) for i in range(peers)])  11.9 us
    ppermute x3, starting transfers between devices, shifted(): lax.ppermute(value, 'pipe', [(i, (i + by) % peers) for i in range(peers)])  8.51 us
    all_to_all x1, starting transfers between devices, summed(): return jnp.sum(lax.all_to_all(parts, 'tensor', 0, 0), axis=0)  5.73 us
    pallas_call x1, Pallas kernels, forward_local(): pl.pallas_call(forward_kernel, in_specs=[pl.BlockSpec(memory_space=pltpu....  4.36 us
    pallas_call x1, Pallas kernels, backward_local(): pl.pallas_call(backward_kernel, in_specs=[whole] * 3, out_specs=[far] * 2...  3.93 us
    ppermute x3, waiting for transfers between devices, shifted(): lax.ppermute(value, 'pipe', [(i, (i + by) % peers) for i in range(peers)])  3.86 us
    all_to_all x1, waiting for transfers between devices, summed(): return jnp.sum(lax.all_to_all(parts, 'tensor', 0, 0), axis=0)  2.77 us
  transfers between devices with their start and end apart: 6, of which 4 were waited for; matrix products, arithmetic and copies ran while one was open for 3% of the time, Pallas kernels for 8%

profile of v4, /device:TPU:122, one launch (start us, length us, event | category | flops | bytes accessed | tf_op | source)
XLA Modules:
  0.0 64.6 jit_solution(15500916078357290616)
XLA Ops:
  0.6 10.0 %collective-permute-start = (bf16[352,1024]{1,0:T(8,128)(2,1)}, bf16[352,1024]{1,0:T(8,128)(2,1)S(1)}, u32[]{:S(2)}, u32[]{:S(2)}) collective-permute-start(bf16[352,1024]{1,0:T(8,128)(2,1)} %bitcast.15), channel_id=1, source_target_pairs={{0,256},{8,264},{16,272},{24,280},{32,288},{40,296},{48,304},{56,3... | collective-permute-start | bytes 2162696 | tf_op jit(solution)/shard_map/ppermute | solution.py:23
  11.3 0.0 copy-start.2
  11.3 4.4 %forward.1 = (bf16[352,1024]{1,0:T(8,128)(2,1)}, f32[352,128]{1,0:T(8,128)}) custom-call(s32[1]{0:T(128)S(6)} %copy.17.b_ref, bf16[352,1024]{1,0:T(8,128)(2,1)} %bitcast.11, bf16[2,352,128]{2,1,0:T(8,128)(2,1)} %bitcast.13, bf16[352,1024]{1,0:T(8,128)(2,1)} %bitcast.12), custom_call_target="tpu_custom_call" | custom-call | flops 1000000 | bytes 100000 | tf_op jit(solution)/shard_map/forward/pallas_call | solution.py:100
  15.7 0.0 copy-start
  15.7 2.1 %collective-permute-start.1 = (bf16[352,1024]{1,0:T(8,128)(2,1)}, bf16[352,1024]{1,0:T(8,128)(2,1)S(1)}, u32[]{:S(2)}, u32[]{:S(2)}) collective-permute-start(bf16[352,1024]{1,0:T(8,128)(2,1)} %get-tuple-element.11), channel_id=1, source_target_pairs={{0,8},{8,16},{16,24},{24,32},{32,40},{40,48},{48,56},{56,64},{64,7... | collective-permute-start | bytes 2162696 | tf_op jit(solution)/shard_map/ppermute | solution.py:18
  17.8 0.0 copy-done.2
  17.8 4.5 %collective-permute-start.4 = (bf16[352,1024]{1,0:T(8,128)(2,1)S(1)}, bf16[352,1024]{1,0:T(8,128)(2,1)S(1)}, u32[]{:S(2)}, u32[]{:S(2)}) collective-permute-start(bf16[352,1024]{1,0:T(8,128)(2,1)S(1)} %bitcast.16), channel_id=1, source_target_pairs={{0,504},{8,0},{16,8},{24,16},{32,24},{40,32},{48,40},{56,48},{64,5... | collective-permute-start | bytes 2162696 | tf_op jit(solution)/shard_map/ppermute | solution.py:18
  22.3 1.1 %reduce_sum.18 = f32[352]{0:T(512)S(1)} reduce(f32[352,128]{1,0:T(8,128)} %get-tuple-element.13, f32[]{:T(128)} %constant.3.clone.1), dimensions={1}, to_apply=%region_0.1 | reduce | flops 44704 | bytes 181636 | tf_op jit(solution)/shard_map/reduce_sum | solution.py:247
  23.4 0.6 broadcast_in_dim.29
  24.0 5.7 %all-to-all-start = ((f32[8,1,352]{2,1,0:T(1,128)}), f32[8,1,352]{2,1,0:T(1,128)S(1)}, u32[]{:S(2)}, u32[]{:S(2)}) async-start(f32[8,1,352]{2,1,0:T(1,128)} %broadcast_in_dim.29), calls=%async_computation | async-start | bytes 24576 | tf_op jit(solution)/shard_map/all_to_all | solution.py:237
  30.4 0.1 pad.1.clone
  30.5 0.0 copy-done
  30.5 0.2 pad_maximum_fusion
  30.6 1.9 %collective-permute-start.3 = (bf16[720,128]{1,0:T(8,128)(2,1)S(1)}, bf16[720,128]{1,0:T(8,128)(2,1)S(1)}, u32[]{:S(2)}, u32[]{:S(2)}) collective-permute-start(bf16[720,128]{1,0:T(8,128)(2,1)S(1)} %pad_maximum_fusion), channel_id=1, source_target_pairs={{0,256},{8,264},{16,272},{24,280},{32,288},{40,296},{48,304},{56,3... | collective-permute-start | bytes 552968 | tf_op jit(solution)/shard_map/ppermute | solution.py:23
  32.6 2.8 %all-to-all-done = f32[8,1,352]{2,1,0:T(1,128)S(1)} async-done(((f32[8,1,352]{2,1,0:T(1,128)}), f32[8,1,352]{2,1,0:T(1,128)S(1)}, u32[]{:S(2)}, u32[]{:S(2)}) %all-to-all-start) | async-done | bytes 11296 | tf_op jit(solution)/shard_map/all_to_all | solution.py:237
  35.4 1.9 %collective-permute-start.2 = (f32[352]{0:T(512)S(1)}, f32[352]{0:T(512)S(1)}, u32[]{:S(2)}, u32[]{:S(2)}) collective-permute-start(f32[352]{0:T(512)S(1)} %add_rsqrt_fusion), channel_id=1, source_target_pairs={{0,8},{8,16},{16,24},{24,32},{32,40},{40,48},{48,56},{56,64},{64,7... | collective-permute-start | bytes 4232 | tf_op jit(solution)/shard_map/ppermute | solution.py:18
  37.3 3.9 %collective-permute-done.2 = f32[352]{0:T(512)S(1)} collective-permute-done((f32[352]{0:T(512)S(1)}, f32[352]{0:T(512)S(1)}, u32[]{:S(2)}, u32[]{:S(2)}) %collective-permute-start.2) | collective-permute-done | bytes 1440 | tf_op jit(solution)/shard_map/ppermute | solution.py:18
  41.2 0.1 broadcast_in_dim.37.scale_ref
  41.3 16.3 %collective-permute-done.after_ref.q_ref = bf16[352,1024]{1,0:T(8,128)(2,1)S(1)} collective-permute-done((bf16[352,1024]{1,0:T(8,128)(2,1)}, bf16[352,1024]{1,0:T(8,128)(2,1)S(1)}, u32[]{:S(2)}, u32[]{:S(2)}) %collective-permute-start) | collective-permute-done | bytes 720928 | tf_op jit(solution)/shard_map/ppermute | solution.py:23
  57.6 0.0 collective-permute-done.1.handed_ref
  57.6 1.0 %finish.1 = bf16[352,1024]{1,0:T(8,128)(2,1)} custom-call(bf16[352,1024]{1,0:T(8,128)(2,1)S(1)} %collective-permute-done.after_ref.q_ref, bf16[352,1024]{1,0:T(8,128)(2,1)S(1)} %collective-permute-done.1.handed_ref, f32[352,1]{1,0:T(8,128)S(1)} %broadcast_in_dim.37.scale_ref, bf16[1,1024]{1,0:T(2,128)(2,1)S(1)} %broadcast_in_dim.31.gain_ref), custom_call_target="tpu_custom_call" | custom-call | flops 1000000000 | tf_op jit(solution)/shard_map/finish/pallas_call | solution.py:219
  58.6 2.1 %collective-permute-done.3.kvb_ref = bf16[720,128]{1,0:T(8,128)(2,1)S(1)} collective-permute-done((bf16[720,128]{1,0:T(8,128)(2,1)S(1)}, bf16[720,128]{1,0:T(8,128)(2,1)S(1)}, u32[]{:S(2)}, u32[]{:S(2)}) %collective-permute-start.3) | collective-permute-done | bytes 184352 | tf_op jit(solution)/shard_map/ppermute | solution.py:23
  60.7 0.0 collective-permute-done.4.g_ref
  60.7 3.9 %backward.1 = (bf16[352,1024]{1,0:T(8,128)(2,1)}, bf16[2,352,128]{2,1,0:T(8,128)(2,1)}) custom-call(bf16[352,1024]{1,0:T(8,128)(2,1)S(1)} %collective-permute-done.after_ref.q_ref, bf16[720,128]{1,0:T(8,128)(2,1)S(1)} %collective-permute-done.3.kvb_ref, bf16[352,1024]{1,0:T(8,128)(2,1)S(1)} %collective-permute-done.4.g_ref), custom_call_target="tpu_custom_call" | custom-call | flops 99999997952 | bytes 3000000 | tf_op jit(solution)/shard_map/backward/pallas_call | solution.py:174
  (6 shorter events, 0.0 us)
Async XLA Ops:
  0.6 57.0 %collective-permute-start = (bf16[352,1024]{1,0:T(8,128)(2,1)}, bf16[352,1024]{1,0:T(8,128)(2,1)S(1)}, u32[]{:S(2)}, u32[]{:S(2)}) collective-permute-start(bf16[352,1024]{1,0:T(8,128)(2,1)} %bitcast.15), channel_id=1, source_target_pairs={{0,256},{8,264},{16,272},{24,280},{32,288},{40,296},{48,304},{56,3... | collective-permute-start | bytes 2162696 | tf_op jit(solution)/shard_map/ppermute | solution.py:23
  11.3 6.5 %copy-start.2 = (bf16[1,352,1024]{2,1,0:T(8,128)(2,1)S(1)}, bf16[1,352,1024]{2,1,0:T(8,128)(2,1)}, u32[]{:S(2)}) copy-start(bf16[1,352,1024]{2,1,0:T(8,128)(2,1)} %param.17) | copy-start | bytes 2162692
  15.7 14.8 %copy-start = (bf16[1,2,352,128]{3,2,1,0:T(8,128)(2,1)S(1)}, bf16[1,2,352,128]{3,2,1,0:T(8,128)(2,1)}, u32[]{:S(2)}) copy-start(bf16[1,2,352,128]{3,2,1,0:T(8,128)(2,1)} %param.15) | copy-start | bytes 540676
  15.7 41.9 %collective-permute-start.1 = (bf16[352,1024]{1,0:T(8,128)(2,1)}, bf16[352,1024]{1,0:T(8,128)(2,1)S(1)}, u32[]{:S(2)}, u32[]{:S(2)}) collective-permute-start(bf16[352,1024]{1,0:T(8,128)(2,1)} %get-tuple-element.11), channel_id=1, source_target_pairs={{0,8},{8,16},{16,24},{24,32},{32,40},{40,48},{48,56},{56,64},{64,7... | collective-permute-start | bytes 2162696 | tf_op jit(solution)/shard_map/ppermute | solution.py:18
  17.8 42.9 %collective-permute-start.4 = (bf16[352,1024]{1,0:T(8,128)(2,1)S(1)}, bf16[352,1024]{1,0:T(8,128)(2,1)S(1)}, u32[]{:S(2)}, u32[]{:S(2)}) collective-permute-start(bf16[352,1024]{1,0:T(8,128)(2,1)S(1)} %bitcast.16), channel_id=1, source_target_pairs={{0,504},{8,0},{16,8},{24,16},{32,24},{40,32},{48,40},{56,48},{64,5... | collective-permute-start | bytes 2162696 | tf_op jit(solution)/shard_map/ppermute | solution.py:18
  24.0 11.3 %all-to-all-start = ((f32[8,1,352]{2,1,0:T(1,128)}), f32[8,1,352]{2,1,0:T(1,128)S(1)}, u32[]{:S(2)}, u32[]{:S(2)}) async-start(f32[8,1,352]{2,1,0:T(1,128)} %broadcast_in_dim.29), calls=%async_computation | async-start | bytes 24576 | tf_op jit(solution)/shard_map/all_to_all | solution.py:237
  30.6 30.1 %collective-permute-start.3 = (bf16[720,128]{1,0:T(8,128)(2,1)S(1)}, bf16[720,128]{1,0:T(8,128)(2,1)S(1)}, u32[]{:S(2)}, u32[]{:S(2)}) collective-permute-start(bf16[720,128]{1,0:T(8,128)(2,1)S(1)} %pad_maximum_fusion), channel_id=1, source_target_pairs={{0,256},{8,264},{16,272},{24,280},{32,288},{40,296},{48,304},{56,3... | collective-permute-start | bytes 552968 | tf_op jit(solution)/shard_map/ppermute | solution.py:23
  35.4 1.9 %copy-start.1 = (bf16[1024]{0:T(1024)(128)(2,1)S(1)}, bf16[1024]{0:T(1024)(128)(2,1)}, u32[]{:S(2)}) copy-start(bf16[1024]{0:T(1024)(128)(2,1)} %param.13) | copy-start | bytes 6148
  35.4 5.8 %collective-permute-start.2 = (f32[352]{0:T(512)S(1)}, f32[352]{0:T(512)S(1)}, u32[]{:S(2)}, u32[]{:S(2)}) collective-permute-start(f32[352]{0:T(512)S(1)} %add_rsqrt_fusion), channel_id=1, source_target_pairs={{0,8},{8,16},{16,24},{24,32},{32,40},{40,48},{48,56},{56,64},{64,7... | collective-permute-start | bytes 4232 | tf_op jit(solution)/shard_map/ppermute | solution.py:18

commit v5 on v4

--- a/solution.py
+++ b/solution.py
@@ -9,6 +9,7 @@
 D = 8192
 BLK = 128
 GROUP = 8
+STEP = 2
 LOG2E = 1.4426950408889634
 NT = (((1,), (1,)), ((), ()))
 
@@ -45,15 +46,18 @@
     return block.astype(jnp.float32).T.astype(jnp.bfloat16)
 
 
-def weights_turned(keys, queries, bias):
-    scores = dot(keys, queries, NT) + jnp.concatenate([bias] * GROUP, axis=1)
+def weights_of(scores):
     top = jnp.max(scores, axis=0, keepdims=True)
     weights = jnp.exp2((scores - top) * (LOG2E * HD**-0.5))
     return weights, 1.0 / jnp.sum(weights, axis=0, keepdims=True)
 
 
-def stacked(ref, start, first, last):
-    heads = [padded(ref[first:last, (start + h) * HD : (start + h + 1) * HD], BLK) for h in range(GROUP)]
+def weights_turned(keys, queries, bias):
+    return weights_of(dot(keys, queries, NT) + jnp.concatenate([bias] * GROUP, axis=1))
+
+
+def stacked(ref, start, first, last, group=GROUP):
+    heads = [padded(ref[first:last, (start + h) * HD : (start + h + 1) * HD], BLK) for h in range(group)]
     return jnp.concatenate(heads, axis=0)
 
 
@@ -135,33 +139,45 @@
     keys_turned = turned(keys)
     digits = kvb_ref[2 * tok :].astype(jnp.float32)
     bound = (digits[0:1] * 16.0 + digits[8:9]).astype(jnp.int32)
-    for n, (first, last, depth) in enumerate(blocks):
-        rows = pl.ds(first, last - first)
-        bias = bias_of(first, depth, bound)
-        for start in range(0, width // HD, GROUP):
-            queries = stacked(q_ref, start, first, last)
-            grads = stacked(g_ref, start, first, last)
-            weights, inverse = weights_turned(keys[:depth], queries, bias)
-            probs = weights * inverse
-            own_v = dot(probs.astype(jnp.bfloat16), grads)
-            grad_p = dot(values[:depth], grads, NT)
-            total = jnp.sum(probs * grad_p, axis=0, keepdims=True)
-            grad_s = (probs * (grad_p - total) * HD**-0.5).astype(jnp.bfloat16)
-            own_k = dot(grad_s, queries)
-            if n == 0 and start == 0:
-                dv_ref[:depth] = own_v
-                dk_ref[:depth] = own_k
-            else:
-                dv_ref[:depth] += own_v
-                dk_ref[:depth] += own_k
-            grad_q = dot(keys_turned[:, :depth], grad_s)
-            for h in range(GROUP):
-                cols = slice((start + h) * HD, (start + h + 1) * HD)
-                dq_ref[first:last, cols] = grad_q[:, h * BLK : (h + 1) * BLK].T[: last - first].astype(jnp.bfloat16)
-        dkv_ref[0, first:last] = dk_ref[first:last].astype(jnp.bfloat16)
-        dkv_ref[1, first:last] = dv_ref[first:last].astype(jnp.bfloat16)
-        leave(dq_ref.at[rows], dq_far.at[rows])
-        leave(dkv_ref.at[:, rows], dkv_far.at[:, rows])
+    steps = [block + (start,) for block in blocks for start in range(0, width // HD, STEP)]
+    biases = {}
+
+    def opened(step):
+        first, last, depth, start = step
+        if first not in biases:
+            biases[first] = bias_of(first, depth, bound)
+        queries = stacked(q_ref, start, first, last, STEP)
+        grads = stacked(g_ref, start, first, last, STEP)
+        scores = dot(keys[:depth], queries, NT) + jnp.concatenate([biases[first]] * STEP, axis=1)
+        return queries, grads, scores, dot(values[:depth], grads, NT)
+
+    ahead = opened(steps[0])
+    for n, (first, last, depth, start) in enumerate(steps):
+        queries, grads, scores, grad_p = ahead
+        if n + 1 < len(steps):
+            ahead = opened(steps[n + 1])
+        weights, inverse = weights_of(scores)
+        probs = weights * inverse
+        own_v = dot(probs.astype(jnp.bfloat16), grads)
+        total = jnp.sum(probs * grad_p, axis=0, keepdims=True)
+        grad_s = (probs * (grad_p - total) * HD**-0.5).astype(jnp.bfloat16)
+        own_k = dot(grad_s, queries)
+        if n == 0:
+            dv_ref[:depth] = own_v
+            dk_ref[:depth] = own_k
+        else:
+            dv_ref[:depth] += own_v
+            dk_ref[:depth] += own_k
+        grad_q = dot(keys_turned[:, :depth], grad_s)
+        for h in range(STEP):
+            cols = slice((start + h) * HD, (start + h + 1) * HD)
+            dq_ref[first:last, cols] = grad_q[:, h * BLK : (h + 1) * BLK].T[: last - first].astype(jnp.bfloat16)
+        if start + STEP == width // HD:
+            rows = pl.ds(first, last - first)
+            dkv_ref[0, first:last] = dk_ref[first:last].astype(jnp.bfloat16)
+            dkv_ref[1, first:last] = dv_ref[first:last].astype(jnp.bfloat16)
+            leave(dq_ref.at[rows], dq_far.at[rows])
+            leave(dkv_ref.at[:, rows], dkv_far.at[:, rows])
     for copy in gone:
         copy.wait()
 

time: 65 us -> 65 us (level)
  no operation moved by 1% of the time
where the time goes in v5:
time: 65 us; the launch traced here: 64.6 us
  starting transfers between devices  26.2 us (40%)
  waiting for transfers between devices  25 us (38%)
  Pallas kernels  9.25 us (14%)
  between operations  2.06 us (3%)
  other arithmetic  1.27 us (2%)
  local copies, waits for them, and re-layouts  0.81 us (1%)
    ppermute x2, waiting for transfers between devices, partner(): lax.ppermute(value, 'pipe', [(i, i ^ peers // 2) for i in range(peers)])  18.4 us
    ppermute x2, starting transfers between devices, partner(): lax.ppermute(value, 'pipe', [(i, i ^ peers // 2) for i in range(peers)])  11.9 us
    ppermute x3, starting transfers between devices, shifted(): lax.ppermute(value, 'pipe', [(i, (i + by) % peers) for i in range(peers)])  8.51 us
    all_to_all x1, starting transfers between devices, summed(): return jnp.sum(lax.all_to_all(parts, 'tensor', 0, 0), axis=0)  5.73 us
    pallas_call x1, Pallas kernels, forward_local(): pl.pallas_call(forward_kernel, in_specs=[pl.BlockSpec(memory_space=pltpu....  4.36 us
    pallas_call x1, Pallas kernels, backward_local(): pl.pallas_call(backward_kernel, in_specs=[whole] * 3, out_specs=[far] * 2...  3.88 us
    ppermute x3, waiting for transfers between devices, shifted(): lax.ppermute(value, 'pipe', [(i, (i + by) % peers) for i in range(peers)])  3.86 us
    all_to_all x1, waiting for transfers between devices, summed(): return jnp.sum(lax.all_to_all(parts, 'tensor', 0, 0), axis=0)  2.77 us
  transfers between devices with their start and end apart: 6, of which 4 were waited for; matrix products, arithmetic and copies ran while one was open for 3% of the time, Pallas kernels for 8%

profile of v5, /device:TPU:122, one launch (start us, length us, event | category | flops | bytes accessed | tf_op | source)
XLA Modules:
  0.0 64.6 jit_solution(9611728236662350913)
XLA Ops:
  0.6 10.0 %collective-permute-start = (bf16[352,1024]{1,0:T(8,128)(2,1)}, bf16[352,1024]{1,0:T(8,128)(2,1)S(1)}, u32[]{:S(2)}, u32[]{:S(2)}) collective-permute-start(bf16[352,1024]{1,0:T(8,128)(2,1)} %bitcast.15), channel_id=1, source_target_pairs={{0,256},{8,264},{16,272},{24,280},{32,288},{40,296},{48,304},{56,3... | collective-permute-start | bytes 2162696 | tf_op jit(solution)/shard_map/ppermute | solution.py:24
  11.3 0.0 copy-start.2
  11.3 4.4 %forward.1 = (bf16[352,1024]{1,0:T(8,128)(2,1)}, f32[352,128]{1,0:T(8,128)}) custom-call(s32[1]{0:T(128)S(6)} %copy.17.b_ref, bf16[352,1024]{1,0:T(8,128)(2,1)} %bitcast.11, bf16[2,352,128]{2,1,0:T(8,128)(2,1)} %bitcast.13, bf16[352,1024]{1,0:T(8,128)(2,1)} %bitcast.12), custom_call_target="tpu_custom_call" | custom-call | flops 1000000 | bytes 100000 | tf_op jit(solution)/shard_map/forward/pallas_call | solution.py:104
  15.7 0.0 copy-start
  15.7 2.1 %collective-permute-start.1 = (bf16[352,1024]{1,0:T(8,128)(2,1)}, bf16[352,1024]{1,0:T(8,128)(2,1)S(1)}, u32[]{:S(2)}, u32[]{:S(2)}) collective-permute-start(bf16[352,1024]{1,0:T(8,128)(2,1)} %get-tuple-element.11), channel_id=1, source_target_pairs={{0,8},{8,16},{16,24},{24,32},{32,40},{40,48},{48,56},{56,64},{64,7... | collective-permute-start | bytes 2162696 | tf_op jit(solution)/shard_map/ppermute | solution.py:19
  17.8 0.0 copy-done.2
  17.8 4.5 %collective-permute-start.4 = (bf16[352,1024]{1,0:T(8,128)(2,1)S(1)}, bf16[352,1024]{1,0:T(8,128)(2,1)S(1)}, u32[]{:S(2)}, u32[]{:S(2)}) collective-permute-start(bf16[352,1024]{1,0:T(8,128)(2,1)S(1)} %bitcast.16), channel_id=1, source_target_pairs={{0,504},{8,0},{16,8},{24,16},{32,24},{40,32},{48,40},{56,48},{64,5... | collective-permute-start | bytes 2162696 | tf_op jit(solution)/shard_map/ppermute | solution.py:19
  22.3 1.1 %reduce_sum.18 = f32[352]{0:T(512)S(1)} reduce(f32[352,128]{1,0:T(8,128)} %get-tuple-element.13, f32[]{:T(128)} %constant.3.clone.1), dimensions={1}, to_apply=%region_0.1 | reduce | flops 44704 | bytes 181636 | tf_op jit(solution)/shard_map/reduce_sum | solution.py:263
  23.4 0.6 broadcast_in_dim.29
  24.0 5.7 %all-to-all-start = ((f32[8,1,352]{2,1,0:T(1,128)}), f32[8,1,352]{2,1,0:T(1,128)S(1)}, u32[]{:S(2)}, u32[]{:S(2)}) async-start(f32[8,1,352]{2,1,0:T(1,128)} %broadcast_in_dim.29), calls=%async_computation | async-start | bytes 24576 | tf_op jit(solution)/shard_map/all_to_all | solution.py:253
  30.4 0.1 pad.1.clone
  30.5 0.0 copy-done
  30.5 0.2 pad_maximum_fusion
  30.6 1.9 %collective-permute-start.3 = (bf16[720,128]{1,0:T(8,128)(2,1)S(1)}, bf16[720,128]{1,0:T(8,128)(2,1)S(1)}, u32[]{:S(2)}, u32[]{:S(2)}) collective-permute-start(bf16[720,128]{1,0:T(8,128)(2,1)S(1)} %pad_maximum_fusion), channel_id=1, source_target_pairs={{0,256},{8,264},{16,272},{24,280},{32,288},{40,296},{48,304},{56,3... | collective-permute-start | bytes 552968 | tf_op jit(solution)/shard_map/ppermute | solution.py:24
  32.6 2.8 %all-to-all-done = f32[8,1,352]{2,1,0:T(1,128)S(1)} async-done(((f32[8,1,352]{2,1,0:T(1,128)}), f32[8,1,352]{2,1,0:T(1,128)S(1)}, u32[]{:S(2)}, u32[]{:S(2)}) %all-to-all-start) | async-done | bytes 11296 | tf_op jit(solution)/shard_map/all_to_all | solution.py:253
  35.4 1.9 %collective-permute-start.2 = (f32[352]{0:T(512)S(1)}, f32[352]{0:T(512)S(1)}, u32[]{:S(2)}, u32[]{:S(2)}) collective-permute-start(f32[352]{0:T(512)S(1)} %add_rsqrt_fusion), channel_id=1, source_target_pairs={{0,8},{8,16},{16,24},{24,32},{32,40},{40,48},{48,56},{56,64},{64,7... | collective-permute-start | bytes 4232 | tf_op jit(solution)/shard_map/ppermute | solution.py:19
  37.3 3.9 %collective-permute-done.2 = f32[352]{0:T(512)S(1)} collective-permute-done((f32[352]{0:T(512)S(1)}, f32[352]{0:T(512)S(1)}, u32[]{:S(2)}, u32[]{:S(2)}) %collective-permute-start.2) | collective-permute-done | bytes 1440 | tf_op jit(solution)/shard_map/ppermute | solution.py:19
  41.2 0.1 broadcast_in_dim.37.scale_ref
  41.3 16.3 %collective-permute-done.after_ref.q_ref = bf16[352,1024]{1,0:T(8,128)(2,1)S(1)} collective-permute-done((bf16[352,1024]{1,0:T(8,128)(2,1)}, bf16[352,1024]{1,0:T(8,128)(2,1)S(1)}, u32[]{:S(2)}, u32[]{:S(2)}) %collective-permute-start) | collective-permute-done | bytes 720928 | tf_op jit(solution)/shard_map/ppermute | solution.py:24
  57.6 0.0 collective-permute-done.1.handed_ref
  57.6 1.0 %finish.1 = bf16[352,1024]{1,0:T(8,128)(2,1)} custom-call(bf16[352,1024]{1,0:T(8,128)(2,1)S(1)} %collective-permute-done.after_ref.q_ref, bf16[352,1024]{1,0:T(8,128)(2,1)S(1)} %collective-permute-done.1.handed_ref, f32[352,1]{1,0:T(8,128)S(1)} %broadcast_in_dim.37.scale_ref, bf16[1,1024]{1,0:T(2,128)(2,1)S(1)} %broadcast_in_dim.31.gain_ref), custom_call_target="tpu_custom_call" | custom-call | flops 1000000000 | tf_op jit(solution)/shard_map/finish/pallas_call | solution.py:235
  58.6 2.1 %collective-permute-done.3.kvb_ref = bf16[720,128]{1,0:T(8,128)(2,1)S(1)} collective-permute-done((bf16[720,128]{1,0:T(8,128)(2,1)S(1)}, bf16[720,128]{1,0:T(8,128)(2,1)S(1)}, u32[]{:S(2)}, u32[]{:S(2)}) %collective-permute-start.3) | collective-permute-done | bytes 184352 | tf_op jit(solution)/shard_map/ppermute | solution.py:24
  60.7 0.0 collective-permute-done.4.g_ref
  60.7 3.9 %backward.1 = (bf16[352,1024]{1,0:T(8,128)(2,1)}, bf16[2,352,128]{2,1,0:T(8,128)(2,1)}) custom-call(bf16[352,1024]{1,0:T(8,128)(2,1)S(1)} %collective-permute-done.after_ref.q_ref, bf16[720,128]{1,0:T(8,128)(2,1)S(1)} %collective-permute-done.3.kvb_ref, bf16[352,1024]{1,0:T(8,128)(2,1)S(1)} %collective-permute-done.4.g_ref), custom_call_target="tpu_custom_call" | custom-call | flops 99999997952 | bytes 3000000 | tf_op jit(solution)/shard_map/backward/pallas_call | solution.py:190
  (6 shorter events, 0.0 us)
Async XLA Ops:
  0.6 57.0 %collective-permute-start = (bf16[352,1024]{1,0:T(8,128)(2,1)}, bf16[352,1024]{1,0:T(8,128)(2,1)S(1)}, u32[]{:S(2)}, u32[]{:S(2)}) collective-permute-start(bf16[352,1024]{1,0:T(8,128)(2,1)} %bitcast.15), channel_id=1, source_target_pairs={{0,256},{8,264},{16,272},{24,280},{32,288},{40,296},{48,304},{56,3... | collective-permute-start | bytes 2162696 | tf_op jit(solution)/shard_map/ppermute | solution.py:24
  11.3 6.5 %copy-start.2 = (bf16[1,352,1024]{2,1,0:T(8,128)(2,1)S(1)}, bf16[1,352,1024]{2,1,0:T(8,128)(2,1)}, u32[]{:S(2)}) copy-start(bf16[1,352,1024]{2,1,0:T(8,128)(2,1)} %param.17) | copy-start | bytes 2162692
  15.7 14.8 %copy-start = (bf16[1,2,352,128]{3,2,1,0:T(8,128)(2,1)S(1)}, bf16[1,2,352,128]{3,2,1,0:T(8,128)(2,1)}, u32[]{:S(2)}) copy-start(bf16[1,2,352,128]{3,2,1,0:T(8,128)(2,1)} %param.15) | copy-start | bytes 540676
  15.7 41.9 %collective-permute-start.1 = (bf16[352,1024]{1,0:T(8,128)(2,1)}, bf16[352,1024]{1,0:T(8,128)(2,1)S(1)}, u32[]{:S(2)}, u32[]{:S(2)}) collective-permute-start(bf16[352,1024]{1,0:T(8,128)(2,1)} %get-tuple-element.11), channel_id=1, source_target_pairs={{0,8},{8,16},{16,24},{24,32},{32,40},{40,48},{48,56},{56,64},{64,7... | collective-permute-start | bytes 2162696 | tf_op jit(solution)/shard_map/ppermute | solution.py:19
  17.8 42.9 %collective-permute-start.4 = (bf16[352,1024]{1,0:T(8,128)(2,1)S(1)}, bf16[352,1024]{1,0:T(8,128)(2,1)S(1)}, u32[]{:S(2)}, u32[]{:S(2)}) collective-permute-start(bf16[352,1024]{1,0:T(8,128)(2,1)S(1)} %bitcast.16), channel_id=1, source_target_pairs={{0,504},{8,0},{16,8},{24,16},{32,24},{40,32},{48,40},{56,48},{64,5... | collective-permute-start | bytes 2162696 | tf_op jit(solution)/shard_map/ppermute | solution.py:19
  24.0 11.3 %all-to-all-start = ((f32[8,1,352]{2,1,0:T(1,128)}), f32[8,1,352]{2,1,0:T(1,128)S(1)}, u32[]{:S(2)}, u32[]{:S(2)}) async-start(f32[8,1,352]{2,1,0:T(1,128)} %broadcast_in_dim.29), calls=%async_computation | async-start | bytes 24576 | tf_op jit(solution)/shard_map/all_to_all | solution.py:253
  30.6 30.1 %collective-permute-start.3 = (bf16[720,128]{1,0:T(8,128)(2,1)S(1)}, bf16[720,128]{1,0:T(8,128)(2,1)S(1)}, u32[]{:S(2)}, u32[]{:S(2)}) collective-permute-start(bf16[720,128]{1,0:T(8,128)(2,1)S(1)} %pad_maximum_fusion), channel_id=1, source_target_pairs={{0,256},{8,264},{16,272},{24,280},{32,288},{40,296},{48,304},{56,3... | collective-permute-start | bytes 552968 | tf_op jit(solution)/shard_map/ppermute | solution.py:24
  35.4 1.9 %copy-start.1 = (bf16[1024]{0:T(1024)(128)(2,1)S(1)}, bf16[1024]{0:T(1024)(128)(2,1)}, u32[]{:S(2)}) copy-start(bf16[1024]{0:T(1024)(128)(2,1)} %param.13) | copy-start | bytes 6148
  35.4 5.8 %collective-permute-start.2 = (f32[352]{0:T(512)S(1)}, f32[352]{0:T(512)S(1)}, u32[]{:S(2)}, u32[]{:S(2)}) collective-permute-start(f32[352]{0:T(512)S(1)} %add_rsqrt_fusion), channel_id=1, source_target_pairs={{0,8},{8,16},{16,24},{24,32},{32,40},{40,48},{48,56},{56,64},{64,7... | collective-permute-start | bytes 4232 | tf_op jit(solution)/shard_map/ppermute | solution.py:19
